TPU v7x, 32 devices: a whole 2x2x4 slice. The times are simulated.
32 devices in a mesh: dp: 32 (over z, y, x, core).
Axes of the slice: x: 2, y: 2, z: 4, core: 2. Of those that a mesh axis runs over, the one named last changes fastest.
Arguments:
- tokens: bfloat16 [100864, 384], P('dp'), may hold values from -6 to 6
- attn_weights: bfloat16 [1536, 384], P('dp')
- expert_in: bfloat16 [3072, 1536], P('dp'), may hold values from -0.3125 to 0.3125
- expert_out: bfloat16 [12288, 384], P('dp'), may hold values from -0.625 to 0.625
- gain_one: float32 [384], replicated, may hold values from 0.5 to 1.5
- gain_two: float32 [384], replicated, may hold values from 0.5 to 1.5
- router: float32 [384, 8], replicated, may hold values from -0.21875 to 0.21875
- routes: int32 [100864, 2], P('dp'), may hold values from 0 to 7, as said below
- slots: int32 [100864, 2], P('dp'), may hold values from 0 to 788, as said below
- cotangent: bfloat16 [100864, 384], P('dp'), may hold values from -6 to 6
Outputs:
- output: bfloat16 [100864, 384], P('dp')
- grad_tokens: bfloat16 [100864, 384], P('dp')
- grad_attn_weights: float32 [1536, 384], P('dp')
- grad_expert_in: float32 [3072, 1536], P('dp')
- grad_expert_out: float32 [12288, 384], P('dp')
- grad_gain_one: float32 [384], replicated
- grad_gain_two: float32 [384], replicated
- grad_router: float32 [384, 8], replicated
Inputs may be any that keep to these rules, and one draw needn't show every extreme that they name: `routes`: the two experts of a token differ. On each device's 3152 tokens, the first choices in token order and then the second choices take the free slots 0, 1, 2 ... of their expert in turn; a pair that finds its expert's 788 slots taken gets 788 and is dropped.
All inputs are finite; a program needn't handle non-finite values.
Results may differ from a plain program's by a relative error of at most 0.012.
Values may be sent and summed in bfloat16 or wider, within the bound.
No kernel may reach another device: no remote copies, remote signals or barrier semaphores. Data moves between devices by JAX's collectives and lax.ppermute only.
A program may use at most 384 MiB of HBM per device.

v0:
```python
import jax
import jax.numpy as jnp
from jax import lax
from jax.sharding import PartitionSpec as P

D = 384
HEADS = 6
FF = 1536
E = 8
SEQ = 197
IMG_DEV = 16
HEAD_DIM = 64
TOK_DEV = 3152
CAP = 788


EPSILON = 1e-06


def layer_norm(values, scale_gain):
    centred = values - jnp.mean(values, axis=-1, keepdims=True)
    spread = jnp.mean(centred * centred, axis=-1, keepdims=True)
    return centred * lax.rsqrt(spread + EPSILON) * scale_gain


def gelu_exact(values):
    return jax.nn.gelu(values, approximate=False)


def route_gates(logit_rows, route_rows):
    chances = jax.nn.softmax(logit_rows, axis=-1)
    picked = (
        route_rows[:, :, None] == jnp.arange(logit_rows.shape[1], dtype=jnp.int32)[None, None, :]
    )
    return jnp.sum(jnp.where(picked, chances[:, None, :], 0.0), axis=-1)


def dispatch_tables(route_rows, slot_rows):
    row_count = route_rows.shape[0]
    slot_index = jnp.where(slot_rows < CAP, route_rows * CAP + slot_rows, E * CAP)
    owners = jnp.broadcast_to(jnp.arange(row_count, dtype=jnp.int32)[:, None], slot_index.shape)
    slot_owner = (
        jnp.full((E * CAP + 1,), row_count, jnp.int32)
        .at[slot_index.reshape(-1)]
        .set(owners.reshape(-1))
    )
    return (slot_owner[: E * CAP], slot_index)


def forward_pass(
    tokens_f, attn_full, in_full, out_full, gain_one, gain_two, router, route_rows, slot_rows
):
    normed_one = layer_norm(tokens_f, gain_one).astype(jnp.bfloat16)

    def project(weight):
        product = jnp.dot(normed_one, weight, preferred_element_type=jnp.float32)
        return product.astype(jnp.bfloat16).reshape(IMG_DEV, SEQ, HEADS, HEAD_DIM)

    queries = project(attn_full[0:D])
    key_rows = project(attn_full[D : 2 * D])
    value_rows = project(attn_full[2 * D : 3 * D])
    scores = jnp.einsum(
        "bqhd,bkhd->bhqk", queries, key_rows, preferred_element_type=jnp.float32
    ) * HEAD_DIM ** (-0.5)
    attn_probs = jax.nn.softmax(scores, axis=-1)
    probs_low = attn_probs.astype(jnp.bfloat16)
    context = jnp.einsum(
        "bhqk,bkhd->bqhd", probs_low, value_rows, preferred_element_type=jnp.float32
    )
    context = context.astype(jnp.bfloat16).reshape(TOK_DEV, D)
    residual = tokens_f + jnp.dot(
        context, attn_full[3 * D : 4 * D], preferred_element_type=jnp.float32
    )
    normed_two = layer_norm(residual, gain_two).astype(jnp.bfloat16)
    logit_rows = jnp.dot(normed_two.astype(jnp.float32), router, precision=lax.Precision.HIGHEST)
    gate_pair = route_gates(logit_rows, route_rows)
    slot_owner, slot_index = dispatch_tables(route_rows, slot_rows)
    padded = jnp.concatenate([normed_two, jnp.zeros((1, D), jnp.bfloat16)], axis=0)
    expert_rows = padded[slot_owner].reshape(E, CAP, D)
    pre_act = jnp.einsum(
        "ecd,edf->ecf", expert_rows, in_full.reshape(E, D, FF), preferred_element_type=jnp.float32
    )
    hidden = gelu_exact(pre_act).astype(jnp.bfloat16)
    returned = jnp.einsum(
        "ecf,efd->ecd", hidden, out_full.reshape(E, FF, D), preferred_element_type=jnp.float32
    )
    flat_out = jnp.concatenate(
        [returned.reshape(E * CAP, D), jnp.zeros((1, D), jnp.float32)], axis=0
    )
    combined = (
        gate_pair[:, 0:1] * flat_out[slot_index[:, 0]]
        + gate_pair[:, 1:2] * flat_out[slot_index[:, 1]]
    )
    return {
        "normed_one": normed_one,
        "queries": queries,
        "key_rows": key_rows,
        "value_rows": value_rows,
        "attn_probs": attn_probs,
        "probs_low": probs_low,
        "context": context,
        "residual": residual,
        "normed_two": normed_two,
        "logit_rows": logit_rows,
        "gate_pair": gate_pair,
        "slot_owner": slot_owner,
        "slot_index": slot_index,
        "expert_rows": expert_rows,
        "pre_act": pre_act,
        "hidden": hidden,
        "flat_out": flat_out,
        "result": residual + combined,
    }


def on_device(
    tokens,
    attn_weights,
    expert_in,
    expert_out,
    gain_one,
    gain_two,
    router,
    routes,
    slots,
    cotangent,
):
    tokens_f = tokens.astype(jnp.float32)
    gathered = (
        lax.all_gather(attn_weights, "dp", axis=0, tiled=True),
        lax.all_gather(expert_in, "dp", axis=0, tiled=True),
        lax.all_gather(expert_out, "dp", axis=0, tiled=True),
    )
    first_pass = forward_pass(
        tokens_f, gathered[0], gathered[1], gathered[2], gain_one, gain_two, router, routes, slots
    )
    output = first_pass["result"].astype(jnp.bfloat16)
    attn_full, in_full, out_full = (
        lax.all_gather(attn_weights, "dp", axis=0, tiled=True),
        lax.all_gather(expert_in, "dp", axis=0, tiled=True),
        lax.all_gather(expert_out, "dp", axis=0, tiled=True),
    )
    saved = forward_pass(
        tokens_f, attn_full, in_full, out_full, gain_one, gain_two, router, routes, slots
    )
    w_in = in_full.reshape(E, D, FF)
    w_out = out_full.reshape(E, FF, D)
    grad_out = cotangent.astype(jnp.float32)
    flat_out = saved["flat_out"]
    slot_index = saved["slot_index"]
    slot_owner = saved["slot_owner"]
    grad_gate = jnp.stack(
        [
            jnp.sum(grad_out * flat_out[slot_index[:, 0]], axis=-1),
            jnp.sum(grad_out * flat_out[slot_index[:, 1]], axis=-1),
        ],
        axis=-1,
    )
    gate_slots = (
        jnp.zeros((E * CAP + 1,), jnp.float32)
        .at[slot_index.reshape(-1)]
        .set(saved["gate_pair"].reshape(-1))[: E * CAP]
    )
    grad_padded = jnp.concatenate([grad_out, jnp.zeros((1, D), jnp.float32)], axis=0)
    grad_returned = (
        (gate_slots[:, None] * grad_padded[slot_owner]).astype(jnp.bfloat16).reshape(E, CAP, D)
    )
    grad_hidden = jnp.einsum(
        "ecd,efd->ecf", grad_returned, w_out, preferred_element_type=jnp.float32
    )
    grad_w_out = jnp.einsum(
        "ecf,ecd->efd", saved["hidden"], grad_returned, preferred_element_type=jnp.float32
    )
    unused_out, gelu_pull = jax.vjp(gelu_exact, saved["pre_act"])
    grad_pre = gelu_pull(grad_hidden)[0].astype(jnp.bfloat16)
    grad_rows = jnp.einsum("ecf,edf->ecd", grad_pre, w_in, preferred_element_type=jnp.float32)
    grad_w_in = jnp.einsum(
        "ecd,ecf->edf", saved["expert_rows"], grad_pre, preferred_element_type=jnp.float32
    )
    grad_in_flat = grad_w_in.reshape(E * D, FF)
    grad_out_flat = grad_w_out.reshape(E * FF, D)
    grad_normed_two = (
        jnp.zeros((TOK_DEV + 1, D), jnp.float32)
        .at[slot_owner]
        .add(grad_rows.reshape(E * CAP, D))[:TOK_DEV]
    )
    unused_gate, gate_pull = jax.vjp(
        lambda logit_part: route_gates(logit_part, routes), saved["logit_rows"]
    )
    grad_logits = gate_pull(grad_gate)[0]
    normed_two_f = saved["normed_two"].astype(jnp.float32)
    grad_router = jnp.einsum(
        "td,te->de", normed_two_f, grad_logits, precision=lax.Precision.HIGHEST
    )
    grad_normed_two = grad_normed_two + jnp.dot(
        grad_logits, router.T, precision=lax.Precision.HIGHEST
    )
    unused_norm, norm_pull = jax.vjp(layer_norm, saved["residual"], gain_two)
    grad_res_norm, grad_gain_two = norm_pull(grad_normed_two)
    grad_residual = grad_out + grad_res_norm
    grad_branch = grad_residual.astype(jnp.bfloat16)
    grad_proj = jnp.einsum(
        "td,tf->df", saved["context"], grad_branch, preferred_element_type=jnp.float32
    )
    grad_context = jnp.dot(
        grad_branch, attn_full[3 * D : 4 * D].T, preferred_element_type=jnp.float32
    )
    grad_context = grad_context.astype(jnp.bfloat16).reshape(IMG_DEV, SEQ, HEADS, HEAD_DIM)
    attn_probs = saved["attn_probs"]
    grad_probs = jnp.einsum(
        "bqhd,bkhd->bhqk", grad_context, saved["value_rows"], preferred_element_type=jnp.float32
    )
    grad_values = jnp.einsum(
        "bhqk,bqhd->bkhd", saved["probs_low"], grad_context, preferred_element_type=jnp.float32
    )
    grad_values = grad_values.astype(jnp.bfloat16).reshape(TOK_DEV, D)
    grad_scores = attn_probs * (
        grad_probs - jnp.sum(grad_probs * attn_probs, axis=-1, keepdims=True)
    )
    grad_scores = grad_scores.astype(jnp.bfloat16)
    grad_queries = jnp.einsum(
        "bhqk,bkhd->bqhd", grad_scores, saved["key_rows"], preferred_element_type=jnp.float32
    ) * HEAD_DIM ** (-0.5)
    grad_queries = grad_queries.astype(jnp.bfloat16).reshape(TOK_DEV, D)
    grad_keys = jnp.einsum(
        "bhqk,bqhd->bkhd", grad_scores, saved["queries"], preferred_element_type=jnp.float32
    ) * HEAD_DIM ** (-0.5)
    grad_keys = grad_keys.astype(jnp.bfloat16).reshape(TOK_DEV, D)
    normed_one = saved["normed_one"]
    grad_attn = jnp.concatenate(
        [
            jnp.einsum("td,tf->df", normed_one, grad_queries, preferred_element_type=jnp.float32),
            jnp.einsum("td,tf->df", normed_one, grad_keys, preferred_element_type=jnp.float32),
            jnp.einsum("td,tf->df", normed_one, grad_values, preferred_element_type=jnp.float32),
            grad_proj,
        ],
        axis=0,
    )
    grad_normed_one = jnp.dot(grad_queries, attn_full[0:D].T, preferred_element_type=jnp.float32)
    grad_normed_one = grad_normed_one + jnp.dot(
        grad_keys, attn_full[D : 2 * D].T, preferred_element_type=jnp.float32
    )
    grad_normed_one = grad_normed_one + jnp.dot(
        grad_values, attn_full[2 * D : 3 * D].T, preferred_element_type=jnp.float32
    )
    unused_first, first_pull = jax.vjp(layer_norm, tokens_f, gain_one)
    grad_tok_norm, grad_gain_one = first_pull(grad_normed_one)
    grad_tokens = (grad_residual + grad_tok_norm).astype(jnp.bfloat16)
    summed_attn, summed_in, summed_out = (
        lax.psum_scatter(grad_attn, "dp", scatter_dimension=0, tiled=True),
        lax.psum_scatter(grad_in_flat, "dp", scatter_dimension=0, tiled=True),
        lax.psum_scatter(grad_out_flat, "dp", scatter_dimension=0, tiled=True),
    )
    small_one, small_two, small_router = lax.psum((grad_gain_one, grad_gain_two, grad_router), "dp")
    return (
        output,
        grad_tokens,
        summed_attn,
        summed_in,
        summed_out,
        small_one,
        small_two,
        small_router,
    )


def solution(mesh):
    in_specs = (
        P("dp", None),
        P("dp", None),
        P("dp", None),
        P("dp", None),
        P(),
        P(),
        P(),
        P("dp", None),
        P("dp", None),
        P("dp", None),
    )
    out_specs = (
        P("dp", None),
        P("dp", None),
        P("dp", None),
        P("dp", None),
        P("dp", None),
        P(),
        P(),
        P(),
    )
    return jax.shard_map(
        on_device, mesh=mesh, in_specs=in_specs, out_specs=out_specs, check_vma=False
    )
```

profile of v0, /device:TPU:0, one launch (start us, length us, event | category | flops | bytes accessed | tf_op | source)
XLA Modules:
  0.0 1231.7 jit_solution(9895188763632879355)
XLA Ops:
  12.0 2.2 convert_reduce_fusion
  16.0 2.5 reshape.198
  19.8 2.2 reshape.248
  22.0 30.4 %scatter_custom_fusion = s32[6305]{0:T(1024)S(1)} fusion(s32[6304]{0:T(1024)S(1)} %fusion.50, s32[6304]{0:T(1024)S(1)} %reshape.248, s32[]{:T(128)} %constant.49.clone.1), kind=kCustom, calls=%fused_computation.124 | custom fusion | bytes 25224 | tf_op jit(solution)/shard_map/scatter | solution.py:45
  52.4 4.3 concatenate.16
  56.7 20.4 %gather_fusion.3 = f32[6304,384]{1,0:T(8,128)} fusion(f32[3153,384]{1,0:T(8,128)} %concatenate.16, s32[7168]{0:T(1024)S(1)} %pad_clamp_fusion), kind=kCustom, calls=%fused_computation.3 | custom fusion | bytes 19391104 | tf_op jit(solution)/shard_map/gather | solution.py:166
  77.1 8.1 gather.21
  85.2 2.7 fusion.23
  88.6 5.0 convolution_convert_fusion.2
  93.6 8.3 reshape.272
  101.9 8.0 copy.59
  109.9 5.0 convolution_convert_fusion.1
  114.9 8.4 reshape.273
  123.3 8.0 copy.60
  131.3 4.9 convolution_convert_fusion.3
  136.2 8.3 reshape.271
  144.6 8.0 copy.61
  152.6 13.2 %fusion.64 = (f32[16,6,197]{2,1,0:T(8,128)S(1)}, f32[16,6,197,197]{2,3,1,0:T(8,128)}) fusion(bf16[16,197,6,64]{1,3,2,0:T(8,128)(2,1)} %copy.59, bf16[16,197,6,64]{1,3,2,0:T(8,128)(2,1)} %copy.60), kind=kOutput, calls=%fused_computation.136 | convolution fusion | flops 488062176 | bytes 19819776 | tf_op jit(solution)/shard_map/sub | solution.py:65
  165.8 9.7 convert_bitcast_fusion.1
  175.6 3.5 copy.63
  179.1 7.0 reshape.197
  186.1 3.7 fusion.65
  195.5 18.3 %gather_fusion = bf16[6304,384]{1,0:T(8,128)(2,1)} fusion(bf16[3153,384]{1,0:T(8,128)(2,1)S(1)} %concatenate.14, s32[7168]{0:T(1024)S(1)} %pad_clamp_fusion), kind=kCustom, calls=%fused_computation | custom fusion | bytes 9708160 | tf_op jit(solution)/shard_map/gather | solution.py:79
  213.7 5.5 reshape.200
  219.2 30.4 %fusion.12 = (u8[788,1536]{1,0:T(8,128)(4,1)S(1)}, u8[788,1536]{1,0:T(8,128)(4,1)S(1)}, f32[8,788,1536]{2,1,0:T(8,128)}) fusion(bf16[8,788,384]{2,1,0:T(8,128)(2,1)} %reshape.200, bf16[8,384,1536]{2,1,0:T(8,128)(2,1)} %bitcast.77), kind=kOutput, calls=%fused_computation.38 | convolution fusion | flops 7559958528 | bytes 55431168 | tf_op jit(solution)/shard_map/ecd,edf->ecf/dot_general | solution.py:80
  249.6 90.3 %multiply_convert_fusion = (bf16[8,788,1536]{2,1,0:T(8,128)(2,1)}, f32[8,788,1536]{2,1,0:T(8,128)}) fusion(f32[8,788,1536]{2,1,0:T(8,128)} %get-tuple-element.34, u8[788,1536]{1,0:T(8,128)(4,1)S(1)} %get-tuple-element.9, u8[788,1536]{1,0:T(8,128)(4,1)S(1)} %get-tuple-element.8), kind=kLoop, calls=%fused_computation.16 | loop fusion | flops 677806080 | bytes 99250176 | tf_op jit(solution)/shard_map/convert_element_type | solution.py:83
  340.0 19.5 %fusion.67 = f32[8,788,384]{2,1,0:T(8,128)} fusion(bf16[8,788,1536]{2,1,0:T(8,128)(2,1)} %get-tuple-element.27, bf16[8,1536,384]{2,1,0:T(8,128)(2,1)} %bitcast.79), kind=kOutput, calls=%fused_computation.139 | convolution fusion | flops 7436500992 | bytes 38486016 | tf_op jit(solution)/shard_map/ecf,efd->ecd/dot_general | solution.py:84
  359.5 7.9 reshape.203
  367.4 8.0 concatenate.15
  375.4 13.7 %gather_fusion.2 = f32[3152,384]{1,0:T(8,128)} fusion(f32[6305,384]{1,0:T(8,128)} %concatenate.15, s32[4096]{0:T(1024)S(1)} %copy-done.53), kind=kCustom, calls=%fused_computation.2 | custom fusion | bytes 9695552 | tf_op jit(solution)/shard_map/gather | solution.py:92
  389.1 13.8 %gather_fusion.1 = f32[3152,384]{1,0:T(8,128)} fusion(f32[6305,384]{1,0:T(8,128)} %concatenate.15, s32[4096]{0:T(1024)S(1)} %copy-done.52), kind=kCustom, calls=%fused_computation.1 | custom fusion | bytes 9695552 | tf_op jit(solution)/shard_map/gather | solution.py:91
  403.0 5.2 multiply_reduce_fusion.5
  410.2 2.2 reshape.256
  412.4 30.0 %scatter_custom_fusion.1 = f32[6305]{0:T(1024)S(1)} fusion(s32[6304]{0:T(1024)} %copy-done.56, f32[6304]{0:T(1024)S(1)} %reshape.256, f32[]{:T(128)} %constant.43.clone.1), kind=kCustom, calls=%fused_computation.122 | custom fusion | bytes 25732 | tf_op jit(solution)/shard_map/scatter | solution.py:162
  442.5 40.6 %add_convert_fusion = bf16[8,788,1536]{2,1,0:T(8,128)(2,1)} fusion(f32[8,788,1536]{2,1,0:T(8,128)} %get-tuple-element.28, f32[8,788,1536]{2,1,0:T(8,128)} %get-tuple-element.34, bf16[8,1536,384]{2,1,0:T(8,128)(2,1)} %bitcast.80, f32[8,788,384]{2,1,0:T(8,128)} %gather.21, f32[8,788]{1,0:T(8,128)S(1)} %mul.271), kind=kOutput, calls=%fused_computation.15 | convolution fusion | flops 7576903680 | bytes 115974784 | tf_op jit(solution)/shard_map/ecd,efd->ecf/dot_general | solution.py:168
  483.2 19.3 %fusion.68 = f32[8,788,384]{2,1,0:T(8,128)} fusion(bf16[8,788,1536]{2,1,0:T(8,128)(2,1)} %add_convert_fusion, bf16[8,384,1536]{2,1,0:T(8,128)(2,1)} %bitcast.78), kind=kOutput, calls=%fused_computation.140 | convolution fusion | flops 7436500992 | bytes 38486016 | tf_op jit(solution)/shard_map/ecf,edf->ecd/dot_general | solution.py:176
  502.4 7.9 reshape.264
  510.3 43.3 %scatter_custom_fusion.2 = f32[3153,384]{1,0:T(8,128)} fusion(s32[6304]{0:T(1024)} %copy-done.50, f32[6304,384]{1,0:T(8,128)} %reshape.264, f32[]{:T(128)} %constant.43.clone.1), kind=kCustom, calls=%fused_computation.82 | custom fusion | flops 2420736 | bytes 4843520 | tf_op jit(solution)/shard_map/scatter-add | solution.py:185
  553.7 10.8 multiply_reduce_fusion.2
  564.5 7.8 fusion.62
  575.9 2.8 convolution_convert_fusion
  578.8 5.3 reshape.274
  584.0 8.0 copy.67
  592.1 12.6 %convert_bitcast_fusion = bf16[16,197,6,64]{1,3,2,0:T(8,128)(2,1)} fusion(bf16[16,197,6,64]{1,3,2,0:T(8,128)(2,1)} %copy.67, f32[16,6,197,197]{2,3,1,0:T(8,128)} %get-tuple-element.31, f32[16,6,197]{2,1,0:T(8,128)S(1)} %copy-done.49), kind=kOutput, calls=%fused_computation.78 | convolution fusion | flops 485546688 | bytes 19819776 | tf_op jit(solution)/shard_map/bhqk,bqhd->bkhd/dot_general | solution.py:213
  604.7 14.5 %multiply_reduce_fusion = (f32[16,6,197]{2,1,0:T(8,128)S(1)}, f32[16,6,197,197]{2,3,1,0:T(8,128)}) fusion(f32[16,6,197,197]{2,3,1,0:T(8,128)} %get-tuple-element.31, f32[16,6,197]{2,1,0:T(8,128)S(1)} %copy-done.49, bf16[16,197,6,64]{1,3,2,0:T(8,128)(2,1)} %copy.67, bf16[16,197,6,64]{1,3,2,0:T(8,128)(2,1)S(1)} %copy-done.23), kind=kOutput, calls=%fused_computation.30 | convolution fusion | flops 488043072 | bytes 34798080 | tf_op jit(solution)/shard_map/bqhd,bkhd->bhqk/dot_general | solution.py:210
  619.2 18.4 %multiply_convert_fusion.1 = bf16[16,6,197,197]{2,3,1,0:T(8,128)(2,1)} fusion(f32[16,6,197,197]{2,3,1,0:T(8,128)} %get-tuple-element.39, f32[16,6,197]{2,1,0:T(8,128)S(1)} %get-tuple-element.38, f32[16,6,197,197]{2,3,1,0:T(8,128)} %get-tuple-element.31, f32[16,6,197]{2,1,0:T(8,128)S(1)} %copy-done.49), kind=kLoop, calls=%fused_computation.29 | loop fusion | flops 14902656 | bytes 37407936 | tf_op jit(solution)/shard_map/convert_element_type | solution.py:220
  637.6 9.8 fusion.28
  647.4 7.6 fusion.27
  655.0 2.3 fusion.72
  659.2 5.8 reshape.209
  665.0 3.8 copy.74
  668.8 5.7 reshape.208
  674.5 5.6 copy.71
  680.1 7.0 reshape.207
  687.1 3.4 fusion.71
  695.4 22.5 %fusion.38 = f32[8,1536,384]{2,1,0:T(8,128)} fusion(bf16[8,788,1536]{2,1,0:T(8,128)(2,1)} %get-tuple-element.27, f32[8,788,384]{2,1,0:T(8,128)} %gather.21, f32[8,788]{1,0:T(8,128)S(1)} %mul.271), kind=kOutput, calls=%fused_computation.85 | convolution fusion | flops 7441342464 | bytes 47948416 | tf_op jit(solution)/shard_map/ecf,ecd->efd/dot_general | solution.py:171
  718.0 21.3 %fusion.73 = f32[8,384,1536]{2,1,0:T(8,128)} fusion(bf16[8,788,384]{2,1,0:T(8,128)(2,1)} %reshape.200, bf16[8,788,1536]{2,1,0:T(8,128)(2,1)} %add_convert_fusion), kind=kOutput, calls=%fused_computation.145 | convolution fusion | flops 7436500992 | bytes 43081728 | tf_op jit(solution)/shard_map/ecd,ecf->edf/dot_general | solution.py:177
  741.0 3.0 fusion.43
  746.7 3.3 fusion.26
  751.2 3.1 fusion.24
  754.3 42.7 %all-reduce.3 = (f32[384]{0:T(512)}, f32[384]{0:T(512)}, f32[384,8]{0,1:T(8,128)}) all-reduce(f32[384]{0:T(512)S(1)} %get-tuple-element.12, f32[384]{0:T(512)S(1)} %copy-done.59, f32[384,8]{0,1:T(8,128)S(1)} %fusion.60), channel_id=1, replica_groups=mesh['dp'=32] {'dp'}, use_global_device_ids=true, to_apply=%region_25.26 | all-reduce | flops 3840 | bytes 30720 | tf_op jit(solution)/shard_map/psum | solution.py:254
  797.1 7.4 add_convert_fusion.1
  804.4 206.6 %reduce-scatter.8.cloned.1.call-done = f32[384,384]{1,0:T(8,128)} async-done(((f32[12288,384]{1,0:T(8,128)}), f32[384,384]{1,0:T(8,128)}) %reduce-scatter.8.cloned.1.call-update) | async-done | bytes 589840 | tf_op jit(solution)/shard_map/reduce_scatter | solution.py:252
  1011.0 213.6 %reduce-scatter.6.cloned.1.call-done = f32[96,1536]{1,0:T(8,128)} async-done(((f32[3072,1536]{1,0:T(8,128)}), f32[96,1536]{1,0:T(8,128)}) %reduce-scatter.6.cloned.1.call-update) | async-done | bytes 589840 | tf_op jit(solution)/shard_map/reduce_scatter | solution.py:251
  (181 shorter events, 31.8 us)
Async XLA Ops:
  7.2 185.8 %copy-start = (f32[384,8]{0,1:T(8,128)S(1)}, f32[384,8]{0,1:T(8,128)}, u32[]{:S(2)}) copy-start(f32[384,8]{0,1:T(8,128)} %param.16) | copy-start | bytes 36868
  7.2 7.0 copy-start.2
  7.2 81.4 %all-gather.4.cloned.1.call-start = ((), (), s32[]{:S(2)}) async-start(), calls=%async_computation.3 | async-start | bytes 1216512 | tf_op jit(solution)/shard_map/all_gather | solution.py:130
  7.9 211.3 %all-gather.6.cloned.1.call-start = ((), (), s32[]{:S(2)}) async-start(), calls=%async_computation.4 | async-start | bytes 9732096 | tf_op jit(solution)/shard_map/all_gather | solution.py:131
  8.7 331.3 %all-gather.8.cloned.1.call-start = ((), (), s32[]{:S(2)}) async-start(), calls=%async_computation.5 | async-start | bytes 9732096 | tf_op jit(solution)/shard_map/all_gather | solution.py:132
  9.4 795.0 %reduce-scatter.4.cloned.1.call-start = ((), (), s32[]{:S(2)}) async-start(), calls=%async_computation.6 | async-start | bytes 2433024 | tf_op jit(solution)/shard_map/reduce_scatter | solution.py:250
  14.2 71.0 %copy-start.29 = (f32[3152]{0:T(1024)}, f32[3152]{0:T(1024)S(1)}, u32[]{:S(2)}) copy-start(f32[3152]{0:T(1024)S(1)} %broadcast_multiply_fusion.1) | copy-start | bytes 37828
  16.0 69.3 %copy-start.38 = (f32[3152]{0:T(1024)}, f32[3152]{0:T(1024)S(1)}, u32[]{:S(2)}) copy-start(f32[3152]{0:T(1024)S(1)} %fusion.51) | copy-start | bytes 37828
  18.6 38.1 %copy-start.56 = (s32[6304]{0:T(1024)}, s32[6304]{0:T(1024)S(1)}, u32[]{:S(2)}) copy-start(s32[6304]{0:T(1024)S(1)} %fusion.50) | copy-start | bytes 75652
  52.4 24.7 %copy-start.50 = (s32[6304]{0:T(1024)}, s32[6304]{0:T(1024)S(1)}, u32[]{:S(2)}) copy-start(s32[6304]{0:T(1024)S(1)} %compare_select_fusion.1) | copy-start | bytes 75652
  77.1 8.1 copy-start.54
  165.8 9.8 copy-start.48
  189.8 3.2 copy-start.1
  189.8 3.2 copy-start.31
  191.0 4.1 copy-start.44
  191.0 4.1 copy-start.36
  193.0 2.2 copy-start.8
  195.1 358.6 %copy-start.20 = (f32[3152,8]{0,1:T(8,128)}, f32[3152,8]{0,1:T(8,128)S(1)}, u32[]{:S(2)}) copy-start(f32[3152,8]{0,1:T(8,128)S(1)} %get-tuple-element.36) | copy-start | bytes 302596
  195.1 358.6 %copy-start.26 = (f32[3152]{0:T(1024)}, f32[3152]{0:T(1024)S(1)}, u32[]{:S(2)}) copy-start(f32[3152]{0:T(1024)S(1)} %get-tuple-element.35) | copy-start | bytes 37828
  195.1 18.6 %copy-start.33 = (f32[3152]{0:T(1024)}, f32[3152]{0:T(1024)S(1)}, u32[]{:S(2)}) copy-start(f32[3152]{0:T(1024)S(1)} %fusion.49) | copy-start | bytes 37828
  367.4 8.1 copy-start.53
  375.4 13.7 %copy-start.52 = (s32[4096]{0:T(1024)S(1)}, s32[4096]{0:T(1024)}, u32[]{:S(2)}) copy-start(s32[4096]{0:T(1024)} %get-tuple-element.43) | copy-start | bytes 49156
  389.1 13.8 %copy-start.7 = (bf16[3152,384]{1,0:T(8,128)(2,1)S(1)}, bf16[3152,384]{1,0:T(8,128)(2,1)}, u32[]{:S(2)}) copy-start(bf16[3152,384]{1,0:T(8,128)(2,1)} %param.19) | copy-start | bytes 7262212
  403.0 5.3 copy-start.51
  408.3 145.3 %copy-start.24 = (f32[3152,8]{0,1:T(8,128)}, f32[3152,8]{0,1:T(8,128)S(1)}, u32[]{:S(2)}) copy-start(f32[3152,8]{0,1:T(8,128)S(1)} %get-tuple-element.16) | copy-start | bytes 302596
  410.2 143.5 %copy-start.40 = (f32[3152]{0:T(1024)}, f32[3152]{0:T(1024)S(1)}, u32[]{:S(2)}) copy-start(f32[3152]{0:T(1024)S(1)} %neg.23) | copy-start | bytes 37828
  510.3 43.3 %copy-start.32 = (f32[3152]{0:T(1024)S(1)}, f32[3152]{0:T(1024)}, u32[]{:S(2)}) copy-start(f32[3152]{0:T(1024)} %copy-done.31) | copy-start | bytes 37828
  510.3 43.4 %copy-start.34 = (f32[3152]{0:T(1024)S(1)}, f32[3152]{0:T(1024)}, u32[]{:S(2)}) copy-start(f32[3152]{0:T(1024)} %copy-done.33) | copy-start | bytes 37828
  510.3 43.4 %copy-start.37 = (f32[3152]{0:T(1024)S(1)}, f32[3152]{0:T(1024)}, u32[]{:S(2)}) copy-start(f32[3152]{0:T(1024)} %copy-done.36) | copy-start | bytes 37828
  510.3 43.4 %copy-start.58 = (f32[384]{0:T(512)S(1)}, f32[384]{0:T(512)}, u32[]{:S(2)}) copy-start(f32[384]{0:T(512)} %param.15) | copy-start | bytes 4612
  510.3 54.2 %slice-start = ((s8[4841472]{0:T(1024)(128)(4,1)}), s8[647168]{0:T(1024)(128)(4,1)S(1)}, s32[]{:S(2)}) async-start(s8[4841472]{0:T(1024)(128)(4,1)} %bitcast.72), calls=%async_computation.9 | async-start | bytes 1294336
  553.7 10.8 copy-start.45
  553.7 10.8 slice-start.1
  572.4 2.1 copy-start.5
  572.4 2.2 copy-start.46
  584.0 8.0 copy-start.49
  592.0 12.6 %copy-start.23 = (bf16[16,197,6,64]{1,3,2,0:T(8,128)(2,1)S(1)}, bf16[16,197,6,64]{1,3,2,0:T(8,128)(2,1)}, u32[]{:S(2)}) copy-start(bf16[16,197,6,64]{1,3,2,0:T(8,128)(2,1)} %copy.61) | copy-start | bytes 7262212
  637.6 9.8 copy-start.10
  647.4 7.7 copy-start.12
  647.4 7.7 copy-start.15
  655.0 2.3 copy-start.22
  674.5 12.6 %copy-start.4 = (bf16[3152,384]{1,0:T(8,128)(2,1)S(1)}, bf16[3152,384]{1,0:T(8,128)(2,1)}, u32[]{:S(2)}) copy-start(bf16[3152,384]{1,0:T(8,128)(2,1)} %fusion.23) | copy-start | bytes 7262212
  687.1 3.4 copy-start.13
  690.5 1.7 copy-start.16
  695.3 315.7 %reduce-scatter.8.cloned.1.call-start = ((), (), s32[]{:S(2)}) async-start(), calls=%async_computation.8 | async-start | bytes 19464192 | tf_op jit(solution)/shard_map/reduce_scatter | solution.py:252
  718.0 506.6 %reduce-scatter.6.cloned.1.call-start = ((), (), s32[]{:S(2)}) async-start(), calls=%async_computation.7 | async-start | bytes 19464192 | tf_op jit(solution)/shard_map/reduce_scatter | solution.py:251
  739.3 1.7 copy-start.17
  741.0 3.0 copy-start.14
  741.0 3.0 copy-start.19
  744.1 2.1 copy-start.3
  744.1 2.5 copy-start.18
  744.1 2.5 copy-start.30
  744.1 2.5 copy-start.55
  746.6 3.4 copy-start.43
  746.6 3.4 copy-start.9
  746.6 3.4 copy-start.21
  746.6 3.4 copy-start.25
  746.6 3.4 copy-start.27
  746.6 3.4 copy-start.35
  746.6 3.4 copy-start.41
  746.7 4.5 copy-start.39
  750.0 4.3 copy-start.6
  750.1 4.2 copy-start.59
  750.1 47.0 %copy-start.47 = (f32[3152]{0:T(1024)S(1)}, f32[3152]{0:T(1024)}, u32[]{:S(2)}) copy-start(f32[3152]{0:T(1024)} %copy-done.46) | copy-start | bytes 37828
  (4 other events, 4.7 us)
Sparse Core Ops, SparseCore 0:
  10.9 56.7 all-gather.3
  70.6 80.9 all-gather.5
  154.5 80.6 all-gather.7
  695.5 101.8 reduce-scatter.3
  805.3 205.7 reduce-scatter.7
  1019.0 205.5 reduce-scatter.5
where the time goes:
time: 1240 us; the launch traced here: 1230 us
  waiting for transfers between devices  422 us (34%)
  local copies, waits for them, and re-layouts  288 us (23%)
  matrix products  274 us (22%)
  other arithmetic  190 us (15%)
  blocking collectives  42.7 us (3%)
  between operations  15.2 us (1%)
    reduce_scatter x1, waiting for transfers between devices, on_device(): lax.psum_scatter(grad_in_flat, 'dp', scatter_dimension=0, tiled=True)  214 us
    reduce_scatter x1, waiting for transfers between devices, on_device(): lax.psum_scatter(grad_out_flat, 'dp', scatter_dimension=0, tiled=True)  207 us
    convert_element_type x1, other arithmetic, forward_pass(): hidden = gelu_exact(pre_act).astype(jnp.bfloat16)  90.3 us
    reshape x6, local copies, waits for them, and re-layouts, project(): return product.astype(jnp.bfloat16).reshape(IMG_DEV, SEQ, HEADS, HEAD_DIM)  49.1 us
    scatter-add x1, other arithmetic, on_device(): grad_normed_two = jnp.zeros((TOK_DEV + 1, D), jnp.float32).at[slot_owner]...  43.3 us
    psum x1, blocking collectives, on_device(): lax.psum((grad_gain_one, grad_gain_two, grad_router), 'dp')  42.7 us
    dot_general x1, matrix products, on_device(): jnp.einsum('ecd,efd->ecf', grad_returned, w_out, preferred_element_type=j...  40.6 us
    dot_general x1, matrix products, forward_pass(): jnp.einsum('ecd,edf->ecf', expert_rows, in_full.reshape(E, D, FF), prefer...  30.4 us
  transfers between devices with their start and end apart: 6, of which 2 were waited for; matrix products, arithmetic and copies ran while one was open for 32% of the time, Pallas kernels for 0%

commit v1 on v0

v1 whole, which is shorter than its diff:
```python
import functools

import jax
import jax.numpy as jnp
from jax import lax
from jax.experimental import pallas as pl
from jax.experimental.pallas import tpu as pltpu
from jax.sharding import PartitionSpec as P

D = 384
HEADS = 6
FF = 1536
E = 8
SEQ = 197
IMG = 16
HD = 64
TOK = 3152
CAP = 788
ROWS = 800
CH = 400
NCH = 8
PAD = CH * NCH
QW = 224
KW = 256
ZERO_SLOT = E * ROWS
EPSILON = 1e-06
NEG = -1e30
F32 = jnp.float32
BF16 = jnp.bfloat16
MIB = 1 << 20
SHARDS = 32
SHARD = 4 * D // SHARDS


def dot_nn(a, b):
    return lax.dot_general(a, b, (((1,), (0,)), ((), ())), preferred_element_type=F32)


def dot_nt(a, b):
    return lax.dot_general(a, b, (((1,), (1,)), ((), ())), preferred_element_type=F32)


def dot_tn(a, b):
    return lax.dot_general(a, b, (((0,), (0,)), ((), ())), preferred_element_type=F32)


def params(limit=60):
    return pltpu.CompilerParams(
        dimension_semantics=("arbitrary",), vmem_limit_bytes=limit * MIB
    )


def normalise(values):
    centred = values - jnp.mean(values, axis=-1, keepdims=True)
    spread = jnp.mean(centred * centred, axis=-1, keepdims=True)
    scale = lax.rsqrt(spread + EPSILON)
    return centred * scale, scale


def norm_pull(n, scale, grad, gain):
    h = grad * gain
    return scale * (
        h - jnp.mean(h, axis=-1, keepdims=True) - n * jnp.mean(h * n, axis=-1, keepdims=True)
    )


def row_mask(step, rows, limit):
    ids = lax.broadcasted_iota(jnp.int32, (rows, 1), 0) + step * rows
    return ids < limit


def whole(shape):
    zeros = (0,) * len(shape)
    return pl.BlockSpec(shape, lambda *_: zeros, pipeline_mode=pl.Buffered(1))


def owners_kernel(idx_ref, out_ref):
    def clear(i, carry):
        for u in range(16):
            out_ref[i * 16 + u] = jnp.int32(PAD)
        return carry

    lax.fori_loop(0, (ZERO_SLOT + 16) // 16, clear, 0)

    def put(i, carry):
        for u in range(8):
            t = i * 8 + u
            out_ref[idx_ref[0, t]] = t
            out_ref[idx_ref[1, t]] = t
        return carry

    lax.fori_loop(0, TOK // 8, put, 0)


def slot_owners(idx):
    return pl.pallas_call(
        owners_kernel,
        out_shape=jax.ShapeDtypeStruct((ZERO_SLOT + 16,), jnp.int32),
        in_specs=[pl.BlockSpec(memory_space=pltpu.SMEM)],
        out_specs=pl.BlockSpec(memory_space=pltpu.SMEM),
        name="slot_owners",
    )(idx)


def project_kernel(at_ref, tok_ref, rel_ref, gain_ref, qkv_ref, w_ref):
    step = pl.program_id(0)

    @pl.when(step == 0)
    def _():
        x, y, core, z = at_ref[0], at_ref[1], at_ref[2], at_ref[3]
        for b in range(SHARDS):
            zb, yb, xb, cb = b // 8, (b // 4) % 2, (b // 2) % 2, b % 2
            j = (cb ^ core) * 16 + (yb ^ y) * 8 + (xb ^ x) * 4 + (zb ^ z)
            w_ref[b * SHARD : (b + 1) * SHARD, :] = rel_ref[j]

    values = jnp.where(row_mask(step, CH, TOK), tok_ref[...].astype(F32), 0.0)
    n, _ = normalise(values)
    normed = (n * gain_ref[...]).astype(BF16)
    for b in range(3):
        cols = dot_nn(normed, w_ref[b * D : (b + 1) * D, :])
        qkv_ref[:, b * D : (b + 1) * D] = cols.astype(BF16)


def project(at, tokens, relative, gain):
    return pl.pallas_call(
        project_kernel,
        grid_spec=pltpu.PrefetchScalarGridSpec(
            num_scalar_prefetch=1,
            grid=(NCH,),
            in_specs=[
                pl.BlockSpec((CH, D), lambda i, a: (i, 0)),
                whole((SHARDS, SHARD, D)),
                whole((1, D)),
            ],
            out_specs=(
                pl.BlockSpec((CH, 3 * D), lambda i, a: (i, 0)),
                whole((4 * D, D)),
            ),
        ),
        out_shape=(
            jax.ShapeDtypeStruct((PAD, 3 * D), BF16),
            jax.ShapeDtypeStruct((4 * D, D), BF16),
        ),
        compiler_params=params(),
        cost_estimate=pl.CostEstimate(flops=2 * TOK * D * D * 3, bytes_accessed=12 * MIB, transcendentals=0),
        name="project",
    )(at, tokens, relative, gain)


def window(image):
    start = image * SEQ
    base = pl.multiple_of((start // 16) * 16, 16)
    return base, start - base


def attend_kernel(qkv_ref, ctx_ref, probs_ref):
    image = pl.program_id(0)
    base, off = window(image)
    keys = lax.broadcasted_iota(jnp.int32, (1, KW), 1)
    key_ok = jnp.logical_and(keys >= off, keys < off + SEQ)
    rows = lax.broadcasted_iota(jnp.int32, (QW, 1), 0)
    row_ok = jnp.logical_and(rows >= off, rows < off + SEQ)
    lanes = lax.broadcasted_iota(jnp.int32, (1, 128), 1)
    for pair in range(HEADS // 2):
        cols = pl.ds(pair * 128, 128)
        q = qkv_ref[pl.ds(base, QW), cols]
        k = qkv_ref[pl.ds(base, KW), pl.ds(D + pair * 128, 128)]
        v = qkv_ref[pl.ds(base, KW), pl.ds(2 * D + pair * 128, 128)]
        total = jnp.zeros((QW, 128), F32)
        for half in range(2):
            mine = jnp.logical_and(lanes >= half * HD, lanes < (half + 1) * HD)
            qh = jnp.where(mine, q, jnp.zeros_like(q))
            vh = jnp.where(mine, v, jnp.zeros_like(v))
            scores = dot_nt(qh, k) * HD ** (-0.5)
            scores = jnp.where(key_ok, scores, NEG)
            top = jnp.max(scores, axis=-1, keepdims=True)
            raw = jnp.exp(scores - top)
            probs = (raw * (1.0 / jnp.sum(raw, axis=-1, keepdims=True))).astype(BF16)
            probs_ref[0, pair * 2 + half] = probs
            total = total + dot_nn(probs, vh)
        old = ctx_ref[pl.ds(base, QW), cols]
        ctx_ref[pl.ds(base, QW), cols] = jnp.where(row_ok, total.astype(BF16), old)


def attend(qkv):
    return pl.pallas_call(
        attend_kernel,
        grid=(IMG,),
        out_shape=(
            jax.ShapeDtypeStruct((PAD, D), BF16),
            jax.ShapeDtypeStruct((IMG, HEADS, QW, KW), BF16),
        ),
        in_specs=[whole((PAD, 3 * D))],
        out_specs=(
            pl.BlockSpec((PAD, D), lambda i: (0, 0), pipeline_mode=pl.Buffered(1)),
            pl.BlockSpec((1, HEADS, QW, KW), lambda i: (i, 0, 0, 0)),
        ),
        compiler_params=params(),
        cost_estimate=pl.CostEstimate(flops=IMG * HEADS * QW * KW * 512, bytes_accessed=24 * MIB, transcendentals=0),
        name="attend",
    )(qkv)


def dispatch_kernel(
    owner_ref, ctx_ref, tok_ref, cot_ref, w_ref, gain_ref, rhi_ref, rlo_ref,
    res_ref, chance_ref, xg_ref, pg_ref, table, picked,
):
    step = pl.program_id(0)
    lanes = lax.broadcasted_iota(jnp.int32, (1, 128), 1)

    @pl.when(step == 0)
    def _():
        table[pl.ds(PAD * 8, 8), :] = jnp.zeros((8, 128), F32)

    @pl.when(step < NCH)
    def _():
        residual = tok_ref[...].astype(F32) + dot_nn(ctx_ref[...], w_ref[...])
        res_ref[...] = residual
        n, _ = normalise(residual)
        normed = (n * gain_ref[...]).astype(BF16)
        logits = dot_nn(normed, rhi_ref[...]) + dot_nn(normed, rlo_ref[...])
        logits = jnp.where(lanes < E, logits, NEG)
        raw = jnp.exp(logits - jnp.max(logits, axis=-1, keepdims=True))
        chances = raw / jnp.sum(raw, axis=-1, keepdims=True)
        chance_ref[...] = chances
        wide = normed.astype(F32)
        cot = cot_ref[...].astype(F32)
        at = pl.multiple_of(step * CH * 8, 8)
        for j in range(3):
            part = slice(j * 128, (j + 1) * 128)
            table[pl.ds(at + j, CH, stride=8), :] = wide[:, part]
            table[pl.ds(at + 3 + j, CH, stride=8), :] = cot[:, part]
        table[pl.ds(at + 6, CH, stride=8), :] = chances

    @pl.when(step >= NCH)
    def _():
        first = (step - NCH) * ROWS

        def pick(i, carry):
            for u in range(32):
                c = i * 32 + u
                row = pl.multiple_of(owner_ref[first + c] * 8, 8)
                picked[pl.ds(pl.multiple_of(c * 8, 8), 8), :] = table[pl.ds(row, 8), :]
            return carry

        lax.fori_loop(0, ROWS // 32, pick, 0)
        for j in range(6):
            xg_ref[0, :, j * 128 : (j + 1) * 128] = picked[pl.ds(j, ROWS, stride=8), :].astype(BF16)
        pg_ref[0] = picked[pl.ds(6, ROWS, stride=8), :]


def dispatch(owner, ctx, tokens, cotangent, weights, gain, rhi, rlo):
    chunk = lambda i, o: (jnp.minimum(i, NCH - 1), 0)
    expert = lambda i, o: (jnp.maximum(i - NCH, 0), 0, 0)
    full = lambda shape: pl.BlockSpec(shape, lambda i, o: (0,) * len(shape), pipeline_mode=pl.Buffered(1))
    return pl.pallas_call(
        dispatch_kernel,
        grid_spec=pltpu.PrefetchScalarGridSpec(
            num_scalar_prefetch=1,
            grid=(NCH + E,),
            in_specs=[
                pl.BlockSpec((CH, D), chunk),
                pl.BlockSpec((CH, D), chunk),
                pl.BlockSpec((CH, D), chunk),
                pl.BlockSpec((D, D), lambda i, o: (3, 0), pipeline_mode=pl.Buffered(1)),
                full((1, D)),
                full((D, 128)),
                full((D, 128)),
            ],
            out_specs=(
                pl.BlockSpec((CH, D), chunk),
                pl.BlockSpec((CH, 128), chunk),
                pl.BlockSpec((1, ROWS, 2 * D), expert),
                pl.BlockSpec((1, ROWS, 128), expert),
            ),
            scratch_shapes=[
                pltpu.VMEM(((PAD + 1) * 8, 128), F32),
                pltpu.VMEM((ROWS * 8, 128), F32),
            ],
        ),
        out_shape=(
            jax.ShapeDtypeStruct((TOK, D), F32),
            jax.ShapeDtypeStruct((TOK, 128), F32),
            jax.ShapeDtypeStruct((E, ROWS, 2 * D), BF16),
            jax.ShapeDtypeStruct((E, ROWS, 128), F32),
        ),
        compiler_params=params(),
        cost_estimate=pl.CostEstimate(flops=2 * TOK * D * D * 10, bytes_accessed=30 * MIB, transcendentals=0),
        name="dispatch",
    )(owner, ctx, tokens, cotangent, weights, gain, rhi, rlo)


A1, A2, A3, A4, A5 = (
    0.5 * 0.254829592, 0.5 * -0.284496736, 0.5 * 1.421413741, 0.5 * -1.453152027, 0.5 * 1.061405429
)


def gelu_parts(u):
    t = 1.0 / (1.0 + (0.3275911 * 0.5**0.5) * jnp.abs(u))
    bell = jnp.exp(-0.5 * (u * u))
    tail = ((((A5 * t + A4) * t + A3) * t + A2) * t + A1) * t * bell
    cdf = jnp.where(u < 0, tail, 1.0 - tail)
    return u * cdf, cdf + u * (bell * 0.3989422804014327)


def expert_kernel(far, at_ref, xg_ref, pg_ref, *refs):
    win, wout = refs[0:8], refs[8:16]
    y_ref, gg_ref = refs[16:18]
    gwin, gwout = refs[18:26], refs[26:34]
    win_s, wout_s, gwin_s, xt_s, gt_s, g_s, ret_s, gr_s = refs[34:]
    step = pl.program_id(0)
    x, y, core, z = at_ref[0], at_ref[1], at_ref[2], at_ref[3]
    rel_y = step % 2
    expert = 2 * ((2 * far + step // 2) ^ z) + (rel_y ^ y)
    place = [((r // 2) ^ x) * 2 + ((r % 2) ^ core) for r in range(4)]
    for side in range(2):

        @pl.when(rel_y == side)
        def _():
            for r in range(4):
                rows = pl.ds(pl.multiple_of(place[r] * 96, 16), 96)
                win_s[rows, :] = win[side * 4 + r][0]
                wout_s[r] = wout[side * 4 + r][0]

    lanes = lax.broadcasted_iota(jnp.int32, (1, 128), 1)
    gate = jnp.sum(jnp.where(lanes == expert, pg_ref[0], 0.0), axis=-1, keepdims=True)
    g_s[...] = (gate * xg_ref[0, :, D:].astype(F32)).astype(BF16)
    xt_s[...] = xg_ref[0, :, :D].T
    gt_s[...] = g_s[...].T
    parts = []
    for r in range(4):
        cols = pl.ds(pl.multiple_of(place[r] * D, 128), D)
        pre = dot_nn(xg_ref[0, :, :D], win_s[:, cols])
        grad_hidden = dot_nt(g_s[...], wout_s[r])
        value, slope = gelu_parts(pre)
        hidden = value.astype(BF16)
        grad_pre = (grad_hidden * slope).astype(BF16)
        ret = dot_nn(hidden, wout_s[r])
        back = dot_nt(grad_pre, win_s[:, cols])
        if r == 0:
            ret_s[...] = ret
            gr_s[...] = back
        else:
            ret_s[...] += ret
            gr_s[...] += back
        parts.append(dot_nn(gt_s[...], hidden).astype(BF16))
        gwin_s[:, cols] = dot_nn(xt_s[...], grad_pre).astype(BF16)
    ret = ret_s[...]
    y_ref[0, :, :D] = (gate * ret).astype(BF16)
    y_ref[0, :, D:] = gr_s[...].astype(BF16)
    grad_gate = jnp.sum(xg_ref[0, :, D:].astype(F32) * ret, axis=-1, keepdims=True)
    gg_ref[0] = jnp.where(lanes == expert, grad_gate, 0.0)
    for side in range(2):

        @pl.when(rel_y == side)
        def _():
            for r in range(4):
                rows = pl.ds(pl.multiple_of(place[r] * 96, 16), 96)
                gwin[side * 4 + r][0] = gwin_s[rows, :]
                gwout[side * 4 + r][0] = parts[r]


def experts(far, at, xg, pg, win, wout):
    group = E // 2
    mine = lambda s, a: (2 * ((2 * far + s // 2) ^ a[3]) + ((s % 2) ^ a[1]), 0, 0)
    step = lambda s, a: (s, 0, 0)
    half = lambda s, a: (s // 2, 0, 0)
    rows_in = D // 4
    return pl.pallas_call(
        functools.partial(expert_kernel, far),
        grid_spec=pltpu.PrefetchScalarGridSpec(
            num_scalar_prefetch=1,
            grid=(group,),
            in_specs=[pl.BlockSpec((1, ROWS, 2 * D), mine), pl.BlockSpec((1, ROWS, 128), mine)]
            + [pl.BlockSpec((1, rows_in, FF), half)] * 8
            + [pl.BlockSpec((1, D, D), half)] * 8,
            out_specs=[pl.BlockSpec((1, ROWS, 2 * D), step), pl.BlockSpec((1, ROWS, 128), step)]
            + [pl.BlockSpec((1, rows_in, FF), half)] * 8
            + [pl.BlockSpec((1, D, D), half)] * 8,
            scratch_shapes=[
                pltpu.VMEM((D, FF), BF16),
                pltpu.VMEM((4, D, D), BF16),
                pltpu.VMEM((D, FF), BF16),
                pltpu.VMEM((D, ROWS), BF16),
                pltpu.VMEM((D, ROWS), BF16),
                pltpu.VMEM((ROWS, D), BF16),
                pltpu.VMEM((ROWS, D), F32),
                pltpu.VMEM((ROWS, D), F32),
            ],
        ),
        out_shape=[
            jax.ShapeDtypeStruct((group, ROWS, 2 * D), BF16),
            jax.ShapeDtypeStruct((group, ROWS, 128), F32),
        ]
        + [jax.ShapeDtypeStruct((group // 2, rows_in, FF), BF16)] * 8
        + [jax.ShapeDtypeStruct((group // 2, D, D), BF16)] * 8,
        compiler_params=params(),
        cost_estimate=pl.CostEstimate(flops=group * 12 * ROWS * D * FF, bytes_accessed=40 * MIB, transcendentals=0),
        name="experts",
    )(at, xg, pg, *win, *wout)


def combine_kernel(
    at_ref, idx_ref, y0_ref, y1_ref, gg0_ref, gg1_ref, res_ref, cot_ref, chance_ref, ctx_ref,
    w_ref, gain_ref, rhi_ref, rlo_ref,
    out_ref, gres_ref, gctx_ref, gwo_ref, ggain_ref, grouter_ref, table, summed,
):
    step = pl.program_id(0)
    group = E // 2

    @pl.when(step == 0)
    def _():
        table[pl.ds(ZERO_SLOT * 8, 8), :] = jnp.zeros((8, 128), F32)

    for rel in range(2):
        y_ref, gg_ref = ((y0_ref, gg0_ref), (y1_ref, gg1_ref))[rel]

        @pl.when(jnp.logical_and(step >= rel * group, step < (rel + 1) * group))
        def _():
            s = step - rel * group
            expert = 2 * ((2 * rel + s // 2) ^ at_ref[3]) + ((s % 2) ^ at_ref[1])
            to = pl.multiple_of(expert * (ROWS * 8), 8)
            for j in range(6):
                table[pl.ds(to + j, ROWS, stride=8), :] = y_ref[0, :, j * 128 : (j + 1) * 128].astype(F32)
            table[pl.ds(to + 6, ROWS, stride=8), :] = gg_ref[0]

    @pl.when(step >= E)
    def _():
        part = step - E
        first = part * CH

        def add(i, carry):
            for u in range(16):
                c = i * 16 + u
                one = pl.multiple_of(idx_ref[0, first + c] * 8, 8)
                two = pl.multiple_of(idx_ref[1, first + c] * 8, 8)
                summed[pl.ds(pl.multiple_of(c * 8, 8), 8), :] = table[pl.ds(one, 8), :] + table[pl.ds(two, 8), :]
            return carry

        lax.fori_loop(0, CH // 16, add, 0)
        ok = row_mask(part, CH, TOK)
        residual = jnp.where(ok, res_ref[...], 0.0)
        cot = jnp.where(ok, cot_ref[...].astype(F32), 0.0)
        chances = jnp.where(ok, chance_ref[...], 0.0)
        ctx = ctx_ref[...]
        ctx = jnp.where(ok, ctx, jnp.zeros_like(ctx))
        pieces = [summed[pl.ds(j, CH, stride=8), :] for j in range(7)]
        out_ref[...] = (residual + jnp.concatenate(pieces[0:3], axis=-1)).astype(BF16)
        grad_chances = pieces[6]
        grad_logits = chances * (
            grad_chances - jnp.sum(grad_chances * chances, axis=-1, keepdims=True)
        )
        high = grad_logits.astype(BF16)
        rest = (grad_logits - high.astype(F32)).astype(BF16)
        grad_normed = jnp.concatenate(pieces[3:6], axis=-1) + (
            dot_nt(high, rhi_ref[...]) + dot_nt(high, rlo_ref[...]) + dot_nt(rest, rhi_ref[...])
        )
        n, scale = normalise(residual)
        gain = gain_ref[...]
        normed = (n * gain).astype(BF16)
        grad_residual = cot + norm_pull(n, scale, grad_normed, gain)
        gres_ref[...] = grad_residual
        branch = jnp.where(ok, grad_residual, 0.0).astype(BF16)
        gctx_ref[...] = dot_nt(branch, w_ref[...]).astype(BF16)
        gwo = dot_tn(ctx, branch)
        ggain = jnp.sum(jnp.where(ok, grad_normed * n, 0.0), axis=0, keepdims=True)
        grouter = dot_tn(normed, high) + dot_tn(normed, rest)

        @pl.when(part == 0)
        def _():
            gwo_ref[...] = gwo
            ggain_ref[...] = ggain
            grouter_ref[...] = grouter

        @pl.when(part > 0)
        def _():
            gwo_ref[...] += gwo
            ggain_ref[...] += ggain
            grouter_ref[...] += grouter


def combine(at, idx, y0, y1, gg0, gg1, res, cot, chances, ctx, weights, gain, rhi, rlo):
    group = E // 2
    chunk = lambda i, *_: (jnp.maximum(i - E, 0), 0)
    full = lambda shape: pl.BlockSpec(shape, lambda i, *_: (0,) * len(shape), pipeline_mode=pl.Buffered(1))
    early = lambda i, *_: (jnp.minimum(i, group - 1), 0, 0)
    late = lambda i, *_: (jnp.clip(i - group, 0, group - 1), 0, 0)
    fixed = lambda shape: pl.BlockSpec(shape, lambda i, *_: (0,) * len(shape))
    return pl.pallas_call(
        combine_kernel,
        grid_spec=pltpu.PrefetchScalarGridSpec(
            num_scalar_prefetch=2,
            grid=(E + NCH,),
            in_specs=[
                pl.BlockSpec((1, ROWS, 2 * D), early),
                pl.BlockSpec((1, ROWS, 2 * D), late),
                pl.BlockSpec((1, ROWS, 128), early),
                pl.BlockSpec((1, ROWS, 128), late),
                pl.BlockSpec((CH, D), chunk),
                pl.BlockSpec((CH, D), chunk),
                pl.BlockSpec((CH, 128), chunk),
                pl.BlockSpec((CH, D), chunk),
                pl.BlockSpec((D, D), lambda i, *_: (3, 0), pipeline_mode=pl.Buffered(1)),
                full((1, D)),
                full((D, 128)),
                full((D, 128)),
            ],
            out_specs=(
                pl.BlockSpec((CH, D), chunk),
                pl.BlockSpec((CH, D), chunk),
                pl.BlockSpec((CH, D), chunk),
                fixed((D, D)),
                fixed((1, D)),
                fixed((D, 128)),
            ),
            scratch_shapes=[
                pltpu.VMEM(((ZERO_SLOT + 1) * 8, 128), F32),
                pltpu.VMEM((CH * 8, 128), F32),
            ],
        ),
        out_shape=(
            jax.ShapeDtypeStruct((TOK, D), BF16),
            jax.ShapeDtypeStruct((TOK, D), F32),
            jax.ShapeDtypeStruct((PAD, D), BF16),
            jax.ShapeDtypeStruct((D, D), F32),
            jax.ShapeDtypeStruct((1, D), F32),
            jax.ShapeDtypeStruct((D, 128), F32),
        ),
        compiler_params=params(),
        cost_estimate=pl.CostEstimate(flops=2 * TOK * D * D * 10, bytes_accessed=36 * MIB, transcendentals=0),
        name="combine",
    )(at, idx, y0, y1, gg0, gg1, res, cot, chances, ctx, weights, gain, rhi, rlo)


def attend_back_kernel(qkv_ref, ctx_ref, gctx_ref, probs_ref, gqkv_ref):
    image = pl.program_id(0)
    base, off = window(image)
    rows = lax.broadcasted_iota(jnp.int32, (QW, 1), 0)
    row_ok = jnp.logical_and(rows >= off, rows < off + SEQ)
    wide = lax.broadcasted_iota(jnp.int32, (KW, 1), 0)
    wide_ok = jnp.logical_and(wide >= off, wide < off + SEQ)
    lanes = lax.broadcasted_iota(jnp.int32, (1, 128), 1)
    scale = HD ** (-0.5)
    for pair in range(HEADS // 2):
        cols = pl.ds(pair * 128, 128)
        cols_k = pl.ds(D + pair * 128, 128)
        cols_v = pl.ds(2 * D + pair * 128, 128)
        q = qkv_ref[pl.ds(base, QW), cols]
        k = qkv_ref[pl.ds(base, KW), cols_k]
        v = qkv_ref[pl.ds(base, KW), cols_v]
        grad = gctx_ref[pl.ds(base, QW), cols]
        grad = jnp.where(row_ok, grad, jnp.zeros_like(grad))
        ctx = ctx_ref[pl.ds(base, QW), cols]
        product = grad.astype(F32) * jnp.where(row_ok, ctx, jnp.zeros_like(ctx)).astype(F32)
        gq = jnp.zeros((QW, 128), F32)
        gk = jnp.zeros((KW, 128), F32)
        gv = jnp.zeros((KW, 128), F32)
        for half in range(2):
            mine = jnp.logical_and(lanes >= half * HD, lanes < (half + 1) * HD)
            grad_h = jnp.where(mine, grad, jnp.zeros_like(grad))
            q_h = jnp.where(mine, q, jnp.zeros_like(q))
            k_h = jnp.where(mine, k, jnp.zeros_like(k))
            mean = jnp.sum(jnp.where(mine, product, 0.0), axis=-1, keepdims=True)
            probs = probs_ref[0, pair * 2 + half]
            grad_probs = dot_nt(grad_h, v)
            grad_scores = (probs.astype(F32) * (grad_probs - mean)).astype(BF16)
            gv = gv + dot_tn(probs, grad_h)
            gq = gq + dot_nn(grad_scores, k_h)
            gk = gk + dot_tn(grad_scores, q_h)
        old = gqkv_ref[pl.ds(base, QW), cols]
        gqkv_ref[pl.ds(base, QW), cols] = jnp.where(row_ok, (gq * scale).astype(BF16), old)
        old = gqkv_ref[pl.ds(base, KW), cols_k]
        gqkv_ref[pl.ds(base, KW), cols_k] = jnp.where(wide_ok, (gk * scale).astype(BF16), old)
        old = gqkv_ref[pl.ds(base, KW), cols_v]
        gqkv_ref[pl.ds(base, KW), cols_v] = jnp.where(wide_ok, gv.astype(BF16), old)


def attend_back(qkv, ctx, gctx, probs):
    return pl.pallas_call(
        attend_back_kernel,
        grid=(IMG,),
        out_shape=jax.ShapeDtypeStruct((PAD, 3 * D), BF16),
        in_specs=[
            whole((PAD, 3 * D)),
            whole((PAD, D)),
            whole((PAD, D)),
            pl.BlockSpec((1, HEADS, QW, KW), lambda i: (i, 0, 0, 0)),
        ],
        out_specs=pl.BlockSpec((PAD, 3 * D), lambda i: (0, 0), pipeline_mode=pl.Buffered(1)),
        compiler_params=params(),
        cost_estimate=pl.CostEstimate(flops=IMG * HEADS * QW * KW * 1024, bytes_accessed=40 * MIB, transcendentals=0),
        name="attend_back",
    )(qkv, ctx, gctx, probs)


def finish_kernel(
    at_ref, tok_ref, gqkv_ref, gres_ref, w_ref, gain_ref, gwo_ref, gtok_ref, rel_ref, ggain_ref, gw_s
):
    step = pl.program_id(0)
    ok = row_mask(step, CH, TOK)
    values = jnp.where(ok, tok_ref[...].astype(F32), 0.0)
    n, scale = normalise(values)
    gain = gain_ref[...]
    normed = (n * gain).astype(BF16)
    gqkv = gqkv_ref[...]
    gqkv = jnp.where(ok, gqkv, jnp.zeros_like(gqkv))
    grad = dot_nt(gqkv[:, 0:D], w_ref[0:D, :])
    for b in range(1, 3):
        grad = grad + dot_nt(gqkv[:, b * D : (b + 1) * D], w_ref[b * D : (b + 1) * D, :])
    gtok_ref[...] = (gres_ref[...] + norm_pull(n, scale, grad, gain)).astype(BF16)
    ggain = jnp.sum(grad * n, axis=0, keepdims=True)
    gw = dot_tn(normed, gqkv)

    @pl.when(step == 0)
    def _():
        gw_s[...] = gw
        ggain_ref[...] = ggain

    @pl.when(step > 0)
    def _():
        gw_s[...] += gw
        ggain_ref[...] += ggain

    @pl.when(step == NCH - 1)
    def _():
        x, y, core, z = at_ref[0], at_ref[1], at_ref[2], at_ref[3]
        for b in range(SHARDS):
            zb, yb, xb, cb = b // 8, (b // 4) % 2, (b // 2) % 2, b % 2
            j = (cb ^ core) * 16 + (yb ^ y) * 8 + (xb ^ x) * 4 + (zb ^ z)
            rows = slice((b % 8) * SHARD, (b % 8 + 1) * SHARD)
            part = gwo_ref[rows, :] if zb == 3 else gw_s[rows, zb * D : (zb + 1) * D]
            rel_ref[j] = part.astype(BF16)


def finish(at, tokens, gqkv, gres, weights, gain, gwo):
    chunk = lambda i, a: (i, 0)
    return pl.pallas_call(
        finish_kernel,
        grid_spec=pltpu.PrefetchScalarGridSpec(
            num_scalar_prefetch=1,
            grid=(NCH,),
            in_specs=[
                pl.BlockSpec((CH, D), chunk),
                pl.BlockSpec((CH, 3 * D), chunk),
                pl.BlockSpec((CH, D), chunk),
                whole((4 * D, D)),
                whole((1, D)),
                whole((D, D)),
            ],
            out_specs=(
                pl.BlockSpec((CH, D), chunk),
                whole((SHARDS, SHARD, D)),
                pl.BlockSpec((1, D), lambda i, a: (0, 0)),
            ),
            scratch_shapes=[pltpu.VMEM((D, 3 * D), F32)],
        ),
        out_shape=(
            jax.ShapeDtypeStruct((TOK, D), BF16),
            jax.ShapeDtypeStruct((SHARDS, SHARD, D), BF16),
            jax.ShapeDtypeStruct((1, D), F32),
        ),
        compiler_params=params(),
        cost_estimate=pl.CostEstimate(flops=2 * TOK * D * D * 6, bytes_accessed=20 * MIB, transcendentals=0),
        name="finish",
    )(at, tokens, gqkv, gres, weights, gain, gwo)


def trade(value, bit, n):
    return lax.ppermute(value, "dp", [(i, i ^ bit) for i in range(n)])


def gather_attn(own, n):
    rel_z = jnp.stack([own] + [trade(own, 8 * j, n) for j in (1, 2, 3)])
    rel_xy = jnp.concatenate([rel_z] + [trade(rel_z, 2 * j, n) for j in (1, 2, 3)])
    return jnp.concatenate([rel_xy, trade(rel_xy, 1, n)])


def gather_group(pair, n):
    from_x = trade(pair, 2, n)
    from_y = trade(pair, 4, n)
    corner = jnp.concatenate([trade(from_x[0:1], 4, n), trade(from_y[1:2], 2, n)])
    gathered = []
    for part in (pair, from_x, from_y, corner):
        gathered += [part, trade(part, 1, n)]
    return gathered


def add_low(*parts):
    total = parts[0].astype(F32)
    for part in parts[1:]:
        total = total + part.astype(F32)
    return total.astype(BF16)


def scatter_group(grads, n):
    near, along_x, along_y, corner = (
        add_low(grads[2 * i], trade(grads[2 * i + 1], 1, n)) for i in range(4)
    )
    via_x = trade(corner[0:1], 2, n)
    via_y = trade(corner[1:2], 4, n)
    along_y = jnp.concatenate([add_low(along_y[0:1], via_x), along_y[1:2]])
    along_x = jnp.concatenate([along_x[0:1], add_low(along_x[1:2], via_y)])
    return add_low(near, trade(along_x, 2, n), trade(along_y, 4, n))


def scatter_z(first, second, n):
    one = trade(first[1], 8, n)
    two = trade(second[0], 16, n)
    three = trade(second[1], 24, n)
    return (first[0].astype(F32) + one.astype(F32)) + (two.astype(F32) + three.astype(F32))


def scatter_attn(rel, n):
    both = add_low(rel[:16], trade(rel[16:], 1, n)).reshape(4, 4, SHARD, D)
    own = add_low(both[0], *[trade(both[j], 2 * j, n) for j in (1, 2, 3)])
    parts = [trade(own[j], 8 * j, n).astype(F32) for j in (1, 2, 3)]
    return (own[0].astype(F32) + parts[0]) + (parts[1] + parts[2])


def sum_all(value, n):
    value = value + trade(value, 1, n)
    value = (value + trade(value, 2, n)) + (trade(value, 4, n) + trade(value, 6, n))
    return (value + trade(value, 8, n)) + (trade(value, 16, n) + trade(value, 24, n))


def split_groups(full, rows):
    parts = full.reshape(4, 2, 2, 2, rows, full.shape[-1])
    return [
        [parts[2 * g : 2 * g + 2, r // 4, (r // 2) % 2, r % 2] for r in range(8)] for g in range(2)
    ]


def join_groups(groups):
    rows, columns = groups[0][0].shape[1:]
    whole_z = [jnp.concatenate([groups[0][r], groups[1][r]]) for r in range(8)]
    return jnp.stack(whole_z, axis=1).reshape(SHARDS, rows, columns)


def on_device(
    n, tokens, attn_weights, expert_in, expert_out, gain_one, gain_two, router, routes, slots,
    cotangent,
):
    placed = n == SHARDS
    if placed:
        me = lax.axis_index("dp")
        at = jnp.stack([(me >> 1) & 1, (me >> 2) & 1, me & 1, me >> 3]).astype(jnp.int32)
        relative = gather_attn(attn_weights, n)
        win, wout = [], []
        for own, into in ((expert_in, win), (expert_out, wout)):
            into.append(gather_group(jnp.stack([own, trade(own, 8, n)]), n))
            into.append(gather_group(jnp.stack([trade(own, 16, n), trade(own, 24, n)]), n))
    else:
        at = jnp.zeros((4,), jnp.int32)
        full = lax.all_gather(attn_weights, "dp", axis=0, tiled=True)
        full = full.reshape(4, 2, 2, 2, SHARD, D)
        relative = full.transpose(3, 1, 2, 0, 4, 5).reshape(SHARDS, SHARD, D)
        win = split_groups(lax.all_gather(expert_in, "dp", axis=0, tiled=True), D // 4)
        wout = split_groups(lax.all_gather(expert_out, "dp", axis=0, tiled=True), D)
    idx = jnp.where(slots < CAP, routes * ROWS + slots, ZERO_SLOT).astype(jnp.int32).T
    idx_pad = jnp.pad(idx, ((0, 0), (0, PAD - TOK)), constant_values=ZERO_SLOT)
    owner = slot_owners(idx)
    wide = jnp.pad(router, ((0, 0), (0, 128 - E)))
    rhi = wide.astype(BF16)
    rlo = (wide - rhi.astype(F32)).astype(BF16)
    one = gain_one.reshape(1, D)
    two = gain_two.reshape(1, D)
    qkv, weights = project(at, tokens, relative, one)
    ctx, probs = attend(qkv)
    res, chances, xg, pg = dispatch(owner, ctx, tokens, cotangent, weights, two, rhi, rlo)
    group = [experts(far, at, xg, pg, win[far], wout[far]) for far in range(2)]
    out, gres, gctx, gwo, ggain_two, grouter = combine(
        at, idx_pad, group[0][0], group[1][0], group[0][1], group[1][1],
        res, cotangent, chances, ctx, weights, two, rhi, rlo,
    )
    gqkv = attend_back(qkv, ctx, gctx, probs)
    gtok, grel, ggain_one = finish(at, tokens, gqkv, gres, weights, one, gwo)
    small = jnp.concatenate([ggain_one, ggain_two, grouter[:, :E].reshape(E, D)])
    if placed:
        gin = scatter_z(*(scatter_group(g[2:10], n) for g in group), n)
        gout = scatter_z(*(scatter_group(g[10:18], n) for g in group), n)
        gattn = scatter_attn(grel, n)
        small = sum_all(small, n)
        gout = gout.T
    else:
        gin = join_groups([g[2:10] for g in group]).reshape(E * D, FF)
        gout = jnp.swapaxes(join_groups([g[10:18] for g in group]), -1, -2).reshape(E * FF, D)
        gattn = grel.reshape(2, 2, 2, 4, SHARD, D).transpose(3, 1, 2, 0, 4, 5).reshape(4 * D, D)
        gin, gout, gattn = (
            lax.psum_scatter(g.astype(F32), "dp", scatter_dimension=0, tiled=True)
            for g in (gin, gout, gattn)
        )
        small = lax.psum(small, "dp")
    return out, gtok, gattn, gin, gout, small[0], small[1], small[2:].reshape(D, E)


def solution(mesh):
    split = P("dp", None)
    return jax.shard_map(
        functools.partial(on_device, mesh.shape["dp"]),
        mesh=mesh,
        in_specs=(split, split, split, split, P(), P(), P(), split, split, split),
        out_specs=(split, split, split, split, split, P(), P(), P()),
        check_vma=False,
    )
```

time: 1240 us -> 586 us (0.47)
  Pallas kernels: 0 us -> 286 us
  matrix products: 274 us -> 0 us
  local copies, waits for them, and re-layouts: 288 us -> 27.1 us
  waiting for transfers between devices: 422 us -> 165 us
  other arithmetic: 190 us -> 13.3 us
  starting transfers between devices: 0.24 us -> 81.6 us
  blocking collectives: 42.7 us -> 0 us
  between operations: 15.2 us -> 2.16 us
    reduce_scatter x3 -> x0, waiting for transfers between devices: 420 us -> none  [the longest x1 214 us: on_device(): lax.psum_scatter(grad_in_flat, 'dp', scatter_dimension=0, tiled=True)]
    pallas_call x0 -> x9, Pallas kernels: none -> 286 us  [the longest x2 111 us: experts(): pl.pallas_call(functools.partial(expert_kernel, far), grid_spec=pltpu.Pre...]
    dot_general x26 -> x0, matrix products: 260 us -> none  [the longest x1 40.6 us: on_device(): jnp.einsum('ecd,efd->ecf', grad_returned, w_out, preferred_element_type=j...]
    ppermute x0 -> x97, waiting for transfers between devices: none -> 165 us  [trade(): return lax.ppermute(value, 'dp', [(i, i ^ bit) for i in range(n)])]
    convert_element_type x6 -> x27, other arithmetic: 122 us -> 6.47 us  [the longest x26 5.81 us: add_low(): return total.astype(BF16)]
    reshape x18 -> x4, local copies, waits for them, and re-layouts: 116 us -> 3.67 us  [the longest x1 1.24 us: on_device(): one = gain_one.reshape(1, D)]
    ppermute x0 -> x97, starting transfers between devices: none -> 81.6 us  [trade(): return lax.ppermute(value, 'dp', [(i, i ^ bit) for i in range(n)])]
    gather x5 -> x0, local copies, waits for them, and re-layouts: 74.3 us -> none  [the longest x2 28.5 us: on_device(): grad_padded[slot_owner]]
  transfers between devices with their start and end apart: 6 -> 97, of which waited for: 2 -> 41; matrix products, arithmetic and copies ran while one was open for 32% -> 6% of each run, Pallas kernels for 0% -> 25%
where the time goes in v1:
time: 586 us; the launch traced here: 575 us
  Pallas kernels  286 us (49%)
  waiting for transfers between devices  165 us (28%)
  starting transfers between devices  81.6 us (14%)
  local copies, waits for them, and re-layouts  27.1 us (5%)
  other arithmetic  13.3 us (2%)
    ppermute x97, waiting for transfers between devices, trade(): return lax.ppermute(value, 'dp', [(i, i ^ bit) for i in range(n)])  165 us
    pallas_call x2, Pallas kernels, experts(): pl.pallas_call(functools.partial(expert_kernel, far), grid_spec=pltpu.Pre...  111 us
    ppermute x97, starting transfers between devices, trade(): return lax.ppermute(value, 'dp', [(i, i ^ bit) for i in range(n)])  81.6 us
    pallas_call x1, Pallas kernels, combine(): pl.pallas_call(combine_kernel, grid_spec=pltpu.PrefetchScalarGridSpec(num...  42.4 us
    pallas_call x1, Pallas kernels, dispatch(): pl.pallas_call(dispatch_kernel, grid_spec=pltpu.PrefetchScalarGridSpec(nu...  30.6 us
    pallas_call x1, Pallas kernels, attend_back(): pl.pallas_call(attend_back_kernel, grid=(IMG,), out_shape=jax.ShapeDtypeS...  27 us
    pallas_call x1, Pallas kernels, attend(): pl.pallas_call(attend_kernel, grid=(IMG,), out_shape=(jax.ShapeDtypeStruc...  25.7 us
    pallas_call x1, Pallas kernels, slot_owners(): pl.pallas_call(owners_kernel, out_shape=jax.ShapeDtypeStruct((ZERO_SLOT +...  19.9 us
  transfers between devices with their start and end apart: 97, of which 41 were waited for; matrix products, arithmetic and copies ran while one was open for 6% of the time, Pallas kernels for 25%

profile of v1, /device:TPU:0, one launch (start us, length us, event | category | flops | bytes accessed | tf_op | source)
XLA Modules:
  0.0 574.9 jit_solution(2258895366728653811)
XLA Ops:
  0.6 3.1 collective-permute-start
  3.7 2.5 collective-permute-start.2
  6.3 2.9 collective-permute-start.36
  9.6 1.4 constant_dynamic-update-slice_fusion.6
  11.8 1.4 fusion.4.idx_ref
  16.4 19.9 %slot_owners.1.owner_ref = s32[6416]{0:T(1024)} custom-call(s32[2,3152]{1,0:T(2,128)} %fusion.4.idx_ref), custom_call_target="tpu_custom_call" | custom-call | tf_op jit(solution)/shard_map/slot_owners/pallas_call | solution.py:96
  37.7 2.5 collective-permute-start.26
  40.9 1.6 collective-permute-start.4
  42.5 1.5 collective-permute-start.3
  45.9 2.2 collective-permute-done.3
  50.6 3.5 collective-permute-done.5
  57.1 8.0 %collective-permute-done.25 = bf16[96,1536]{1,0:T(8,128)(2,1)S(1)} collective-permute-done((bf16[96,1536]{1,0:T(8,128)(2,1)S(1)}, bf16[96,1536]{1,0:T(8,128)(2,1)S(1)}, u32[]{:S(2)}, u32[]{:S(2)}) %collective-permute-start.25) | collective-permute-done | bytes 294944 | tf_op jit(solution)/shard_map/ppermute | solution.py:669
  65.1 1.5 collective-permute-start.38
  68.0 3.2 collective-permute-done.16
  71.1 1.5 collective-permute-start.28
  75.7 5.7 collective-permute-done.38.refs_10_
  81.4 1.5 collective-permute-start.30
  83.4 10.6 %collective-permute-done.28.refs_2_ = bf16[2,96,1536]{2,1,0:T(8,128)(2,1)S(1)} collective-permute-done((bf16[2,96,1536]{2,1,0:T(8,128)(2,1)S(1)}, bf16[2,96,1536]{2,1,0:T(8,128)(2,1)S(1)}, u32[]{:S(2)}, u32[]{:S(2)}) %collective-permute-start.28) | collective-permute-done | bytes 589856 | tf_op jit(solution)/shard_map/ppermute | solution.py:669
  94.0 1.5 collective-permute-start.9
  96.4 12.0 %project.1 = (bf16[3200,1152]{1,0:T(8,128)(2,1)}, bf16[1536,384]{1,0:T(8,128)(2,1)}) custom-call(s32[4]{0:T(128)} %pad_add_fusion.at_ref, bf16[3152,384]{1,0:T(8,128)(2,1)} %tok_ref.5, bf16[32,48,384]{2,1,0:T(8,128)(2,1)} %constant_dynamic-update-slice_fusion.7.rel_ref, f32[1,384]{1,0:T(1,128)} %reshape.43.gain_ref), custom_call_target="tpu_custom_call" | custom-call | flops 2788687872 | bytes 12582912 | tf_op jit(solution)/shard_map/project/pallas_call | solution.py:125
  108.4 25.7 %attend.1 = (bf16[3200,384]{1,0:T(8,128)(2,1)}, bf16[16,6,224,256]{3,2,1,0:T(8,128)(2,1)}) custom-call(bf16[3200,1152]{1,0:T(8,128)(2,1)} %get-tuple-element.61.qkv_ref), custom_call_target="tpu_custom_call" | custom-call | flops 2818572288 | bytes 25165824 | tf_op jit(solution)/shard_map/attend/pallas_call | solution.py:186
  134.9 1.5 collective-permute-start.42
  136.9 30.6 %dispatch.1 = (f32[3152,384]{1,0:T(8,128)}, f32[3152,128]{1,0:T(8,128)}, bf16[8,800,768]{2,1,0:T(8,128)(2,1)}, f32[8,800,128]{2,1,0:T(8,128)}) custom-call(s32[6416]{0:T(1024)} %slot_owners.1.owner_ref, bf16[3200,384]{1,0:T(8,128)(2,1)} %get-tuple-element.62.ctx_ref, bf16[3152,384]{1,0:T(8,128)(2,1)} %tok_ref.5, bf16[3152,384]{1,0:T(8,128)(2,1)} %cot_ref.3, ...), custom_call_target="tpu_custom_call" | custom-call | flops 9295626240 | bytes 31457280 | tf_op jit(solution)/shard_map/dispatch/pallas_call | solution.py:256
  175.2 6.4 %collective-permute-done.43 = bf16[1,384,384]{2,1,0:T(8,128)(2,1)S(1)} collective-permute-done((bf16[1,384,384]{2,1,0:T(8,128)(2,1)S(1)}, bf16[1,384,384]{2,1,0:T(8,128)(2,1)S(1)}, u32[]{:S(2)}, u32[]{:S(2)}) %collective-permute-start.43) | collective-permute-done | bytes 294944 | tf_op jit(solution)/shard_map/ppermute | solution.py:669
  181.6 1.5 collective-permute-start.22
  183.2 4.8 collective-permute-done.23
  188.8 5.5 collective-permute-done.33
  194.3 1.5 collective-permute-start.13
  196.0 3.5 collective-permute-done.14
  199.5 1.6 collective-permute-done.13
  204.1 1.5 collective-permute-done.34.refs_7_
  206.4 55.5 %experts.3 = (bf16[4,800,768]{2,1,0:T(8,128)(2,1)}, f32[4,800,128]{2,1,0:T(8,128)}, bf16[2,96,1536]{2,1,0:T(8,128)(2,1)}, bf16[2,96,1536]{2,1,0:T(8,128)(2,1)}, ...) custom-call(s32[4]{0:T(128)} %pad_add_fusion.at_ref, ...), custom_call_target="tpu_custom_call" | custom-call | flops 22649241600 | bytes 41943040 | tf_op jit(solution)/shard_map/experts/pallas_call | solution.py:369
  263.2 55.9 %experts.2 = (bf16[4,800,768]{2,1,0:T(8,128)(2,1)}, f32[4,800,128]{2,1,0:T(8,128)}, bf16[2,96,1536]{2,1,0:T(8,128)(2,1)}, bf16[2,96,1536]{2,1,0:T(8,128)(2,1)}, ...) custom-call(s32[4]{0:T(128)} %pad_add_fusion.at_ref, ...), custom_call_target="tpu_custom_call" | custom-call | flops 22649241600 | bytes 41943040 | tf_op jit(solution)/shard_map/experts/pallas_call | solution.py:369
  319.1 42.4 %combine.1 = (bf16[3152,384]{1,0:T(8,128)(2,1)}, f32[3152,384]{1,0:T(8,128)}, bf16[3200,384]{1,0:T(8,128)(2,1)}, f32[384,384]{1,0:T(8,128)}, f32[1,384]{1,0:T(1,128)}, /*index=5*/f32[384,128]{1,0:T(8,128)}) custom-call(s32[4]{0:T(128)} %pad_add_fusion.at_ref, s32[2,3200]{1,0:T(2,128)} %pad.8.idx_ref, bf16[4,800,768]{2,1,0:T(8,128)(2,1)} %get-tuple-element.66.y0_ref, ...), custom_call_target="tpu_custom_call" | custom-call | flops 9295626240 | bytes 37748736 | tf_op jit(solution)/shard_map/combine/pallas_call | solution.py:489
  362.5 27.0 %attend_back.1.gqkv_ref = bf16[3200,1152]{1,0:T(8,128)(2,1)} custom-call(bf16[3200,1152]{1,0:T(8,128)(2,1)} %get-tuple-element.61.qkv_ref, bf16[3200,384]{1,0:T(8,128)(2,1)} %get-tuple-element.62.ctx_ref, bf16[3200,384]{1,0:T(8,128)(2,1)} %get-tuple-element.73.gctx_ref, bf16[16,6,224,256]{3,2,1,0:T(8,128)(2,1)} %get-tuple-element.74.probs_ref), custom_call_target="tpu_custom_call" | custom-call | flops 5637144576 | bytes 41943040 | tf_op jit(solution)/shard_map/attend_back/pallas_call | solution.py:579
  389.5 16.7 %finish.1 = (bf16[3152,384]{1,0:T(8,128)(2,1)}, bf16[32,48,384]{2,1,0:T(8,128)(2,1)}, f32[1,384]{1,0:T(1,128)}) custom-call(s32[4]{0:T(128)} %pad_add_fusion.at_ref, bf16[3152,384]{1,0:T(8,128)(2,1)} %tok_ref.5, bf16[3200,1152]{1,0:T(8,128)(2,1)} %attend_back.1.gqkv_ref, f32[3152,384]{1,0:T(8,128)} %get-tuple-element.75.gres_ref, ...), custom_call_target="tpu_custom_call" | custom-call | flops 5577375744 | bytes 20971520 | tf_op jit(solution)/shard_map/finish/pallas_call | solution.py:637
  408.9 1.8 collective-permute-start.93
  415.2 2.7 collective-permute-start.96
  417.8 1.8 collective-permute-start.94
  419.6 1.9 slice.175
  424.7 1.7 collective-permute-done.63
  436.7 2.1 collective-permute-start.48
  441.6 1.7 collective-permute-start.64
  443.3 1.9 collective-permute-done.48
  446.4 2.0 collective-permute-done.47
  449.0 5.7 collective-permute-done.64
  456.7 4.4 collective-permute-done.83
  462.1 4.7 collective-permute-done.55
  470.2 5.0 collective-permute-done.74
  476.2 1.5 collective-permute-done.77
  478.9 11.4 %collective-permute-done.65 = bf16[2,96,1536]{2,1,0:T(8,128)(2,1)S(1)} collective-permute-done((bf16[2,96,1536]{2,1,0:T(8,128)(2,1)S(1)}, bf16[2,96,1536]{2,1,0:T(8,128)(2,1)S(1)}, u32[]{:S(2)}, u32[]{:S(2)}) %collective-permute-start.65) | collective-permute-done | bytes 589856 | tf_op jit(solution)/shard_map/ppermute | solution.py:669
  490.3 1.4 collective-permute-start.87
  492.7 1.4 add_convert_fusion.10
  494.9 8.1 %collective-permute-done.84 = bf16[2,384,384]{2,1,0:T(8,128)(2,1)S(1)} collective-permute-done((bf16[2,384,384]{2,1,0:T(8,128)(2,1)S(1)}, bf16[2,384,384]{2,1,0:T(8,128)(2,1)S(1)}, u32[]{:S(2)}, u32[]{:S(2)}) %collective-permute-start.84) | collective-permute-done | bytes 589856 | tf_op jit(solution)/shard_map/ppermute | solution.py:669
  503.0 3.6 collective-permute-done.87
  507.9 1.5 collective-permute-start.78
  509.4 6.1 %collective-permute-done.56 = bf16[2,96,1536]{2,1,0:T(8,128)(2,1)S(1)} collective-permute-done((bf16[2,96,1536]{2,1,0:T(8,128)(2,1)S(1)}, bf16[2,96,1536]{2,1,0:T(8,128)(2,1)S(1)}, u32[]{:S(2)}, u32[]{:S(2)}) %collective-permute-start.56) | collective-permute-done | bytes 589856 | tf_op jit(solution)/shard_map/ppermute | solution.py:669
  515.9 3.3 collective-permute-done.59
  519.2 3.4 collective-permute-start.51
  523.0 3.6 collective-permute-done.75
  527.6 3.5 collective-permute-start.89
  532.5 3.4 collective-permute-start.70
  535.9 23.0 %collective-permute-done.88 = bf16[384,384]{1,0:T(8,128)(2,1)S(1)} collective-permute-done((bf16[384,384]{1,0:T(8,128)(2,1)S(1)}, bf16[384,384]{1,0:T(8,128)(2,1)S(1)}, u32[]{:S(2)}, u32[]{:S(2)}) %collective-permute-start.88) | collective-permute-done | bytes 294944 | tf_op jit(solution)/shard_map/ppermute | solution.py:669
  560.8 12.9 %collective-permute-done.69 = bf16[96,1536]{1,0:T(8,128)(2,1)S(1)} collective-permute-done((bf16[96,1536]{1,0:T(8,128)(2,1)S(1)}, bf16[96,1536]{1,0:T(8,128)(2,1)S(1)}, u32[]{:S(2)}, u32[]{:S(2)}) %collective-permute-start.69) | collective-permute-done | bytes 294944 | tf_op jit(solution)/shard_map/ppermute | solution.py:669
  (374 shorter events, 77.7 us)
Async XLA Ops:
  0.6 37.0 %collective-permute-start = (bf16[48,384]{1,0:T(8,128)(2,1)}, bf16[48,384]{1,0:T(8,128)(2,1)S(1)}, u32[]{:S(2)}, u32[]{:S(2)}) collective-permute-start(bf16[48,384]{1,0:T(8,128)(2,1)} %param.11), channel_id=1, source_target_pairs={{0,8},{1,9},{2,10},{3,11},{4,12},{5,13},{6,14},{7,15},{8,0},{9,1},... | collective-permute-start | bytes 110600 | tf_op jit(solution)/shard_map/ppermute | solution.py:669
  3.7 36.4 %collective-permute-start.2 = (bf16[48,384]{1,0:T(8,128)(2,1)}, bf16[48,384]{1,0:T(8,128)(2,1)S(1)}, u32[]{:S(2)}, u32[]{:S(2)}) collective-permute-start(bf16[48,384]{1,0:T(8,128)(2,1)} %param.11), channel_id=1, source_target_pairs={{0,24},{1,25},{2,26},{3,27},{4,28},{5,29},{6,30},{7,31},{8,16},{9,... | collective-permute-start | bytes 110600 | tf_op jit(solution)/shard_map/ppermute | solution.py:669
  6.2 33.9 %collective-permute-start.1 = (bf16[48,384]{1,0:T(8,128)(2,1)}, bf16[48,384]{1,0:T(8,128)(2,1)S(1)}, u32[]{:S(2)}, u32[]{:S(2)}) collective-permute-start(bf16[48,384]{1,0:T(8,128)(2,1)} %param.11), channel_id=1, source_target_pairs={{0,16},{1,17},{2,18},{3,19},{4,20},{5,21},{6,22},{7,23},{8,24},{9,... | collective-permute-start | bytes 110600 | tf_op jit(solution)/shard_map/ppermute | solution.py:669
  6.3 49.4 %collective-permute-start.36 = (bf16[384,384]{1,0:T(8,128)(2,1)}, bf16[384,384]{1,0:T(8,128)(2,1)S(1)}, u32[]{:S(2)}, u32[]{:S(2)}) collective-permute-start(bf16[384,384]{1,0:T(8,128)(2,1)} %param.13), channel_id=1, source_target_pairs={{0,24},{1,25},{2,26},{3,27},{4,28},{5,29},{6,30},{7,31},{8,16},{9,... | collective-permute-start | bytes 884744 | tf_op jit(solution)/shard_map/ppermute | solution.py:669
  9.2 47.6 %collective-permute-start.35 = (bf16[384,384]{1,0:T(8,128)(2,1)}, bf16[384,384]{1,0:T(8,128)(2,1)S(1)}, u32[]{:S(2)}, u32[]{:S(2)}) collective-permute-start(bf16[384,384]{1,0:T(8,128)(2,1)} %param.13), channel_id=1, source_target_pairs={{0,16},{1,17},{2,18},{3,19},{4,20},{5,21},{6,22},{7,23},{8,24},{9,... | collective-permute-start | bytes 884744 | tf_op jit(solution)/shard_map/ppermute | solution.py:669
  37.7 19.3 %collective-permute-start.26 = (bf16[96,1536]{1,0:T(8,128)(2,1)}, bf16[96,1536]{1,0:T(8,128)(2,1)S(1)}, u32[]{:S(2)}, u32[]{:S(2)}) collective-permute-start(bf16[96,1536]{1,0:T(8,128)(2,1)} %param.12), channel_id=1, source_target_pairs={{0,24},{1,25},{2,26},{3,27},{4,28},{5,29},{6,30},{7,31},{8,16},{9,... | collective-permute-start | bytes 884744 | tf_op jit(solution)/shard_map/ppermute | solution.py:669
  49.8 15.3 %collective-permute-start.25 = (bf16[96,1536]{1,0:T(8,128)(2,1)S(1)}, bf16[96,1536]{1,0:T(8,128)(2,1)S(1)}, u32[]{:S(2)}, u32[]{:S(2)}) collective-permute-start(bf16[96,1536]{1,0:T(8,128)(2,1)S(1)} %copy-done.26), channel_id=1, source_target_pairs={{0,16},{1,17},{2,18},{3,19},{4,20},{5,21},{6,22},{7,23},{8,24},{9,... | collective-permute-start | bytes 884744 | tf_op jit(solution)/shard_map/ppermute | solution.py:669
  54.1 13.8 %collective-permute-start.7 = (bf16[96,1536]{1,0:T(8,128)(2,1)S(1)}, bf16[96,1536]{1,0:T(8,128)(2,1)S(1)}, u32[]{:S(2)}, u32[]{:S(2)}) collective-permute-start(bf16[96,1536]{1,0:T(8,128)(2,1)S(1)} %copy-done.26), channel_id=1, source_target_pairs={{0,8},{1,9},{2,10},{3,11},{4,12},{5,13},{6,14},{7,15},{8,0},{9,1},... | collective-permute-start | bytes 884744 | tf_op jit(solution)/shard_map/ppermute | solution.py:669
  55.7 15.4 %collective-permute-start.16 = (bf16[384,384]{1,0:T(8,128)(2,1)S(1)}, bf16[384,384]{1,0:T(8,128)(2,1)S(1)}, u32[]{:S(2)}, u32[]{:S(2)}) collective-permute-start(bf16[384,384]{1,0:T(8,128)(2,1)S(1)} %copy-done.25), channel_id=1, source_target_pairs={{0,8},{1,9},{2,10},{3,11},{4,12},{5,13},{6,14},{7,15},{8,0},{9,1},... | collective-permute-start | bytes 884744 | tf_op jit(solution)/shard_map/ppermute | solution.py:669
  56.9 17.3 %collective-permute-start.6 = (bf16[16,48,384]{2,1,0:T(8,128)(2,1)S(1)}, bf16[16,48,384]{2,1,0:T(8,128)(2,1)S(1)}, u32[]{:S(2)}, u32[]{:S(2)}) collective-permute-start(bf16[16,48,384]{2,1,0:T(8,128)(2,1)S(1)} %get-tuple-element.150), channel_id=1, source_target_pairs={{0,1},{1,0},{2,3},{3,2},{4,5},{5,4},{6,7},{7,6},{8,9},{9,8},{10,11... | collective-permute-start | bytes 1769480 | tf_op jit(solution)/shard_map/ppermute | solution.py:669
  57.0 18.2 %collective-permute-start.40 = (bf16[2,384,384]{2,1,0:T(8,128)(2,1)S(1)}, bf16[2,384,384]{2,1,0:T(8,128)(2,1)S(1)}, u32[]{:S(2)}, u32[]{:S(2)}) collective-permute-start(bf16[2,384,384]{2,1,0:T(8,128)(2,1)S(1)} %pad_maximum_fusion.3.refs_8_), channel_id=1, source_target_pairs={{0,4},{1,5},{2,6},{3,7},{4,0},{5,1},{6,2},{7,3},{8,12},{9,13},{10,... | collective-permute-start | bytes 1769480 | tf_op jit(solution)/shard_map/ppermute | solution.py:669
  65.1 16.3 %collective-permute-start.38 = (bf16[2,384,384]{2,1,0:T(8,128)(2,1)S(1)}, bf16[2,384,384]{2,1,0:T(8,128)(2,1)S(1)}, u32[]{:S(2)}, u32[]{:S(2)}) collective-permute-start(bf16[2,384,384]{2,1,0:T(8,128)(2,1)S(1)} %pad_maximum_fusion.3.refs_8_), channel_id=1, source_target_pairs={{0,2},{1,3},{2,0},{3,1},{4,6},{5,7},{6,4},{7,5},{8,10},{9,11},{10,... | collective-permute-start | bytes 1769480 | tf_op jit(solution)/shard_map/ppermute | solution.py:669
  68.0 14.9 %collective-permute-start.37 = (bf16[2,384,384]{2,1,0:T(8,128)(2,1)S(1)}, bf16[2,384,384]{2,1,0:T(8,128)(2,1)S(1)}, u32[]{:S(2)}, u32[]{:S(2)}) collective-permute-start(bf16[2,384,384]{2,1,0:T(8,128)(2,1)S(1)} %pad_maximum_fusion.3.refs_8_), channel_id=1, source_target_pairs={{0,1},{1,0},{2,3},{3,2},{4,5},{5,4},{6,7},{7,6},{8,9},{9,8},{10,11... | collective-permute-start | bytes 1769480 | tf_op jit(solution)/shard_map/ppermute | solution.py:669
  71.1 22.9 %collective-permute-start.28 = (bf16[2,96,1536]{2,1,0:T(8,128)(2,1)S(1)}, bf16[2,96,1536]{2,1,0:T(8,128)(2,1)S(1)}, u32[]{:S(2)}, u32[]{:S(2)}) collective-permute-start(bf16[2,96,1536]{2,1,0:T(8,128)(2,1)S(1)} %pad_maximum_fusion.2.refs_0_), channel_id=1, source_target_pairs={{0,2},{1,3},{2,0},{3,1},{4,6},{5,7},{6,4},{7,5},{8,10},{9,11},{10,... | collective-permute-start | bytes 1769480 | tf_op jit(solution)/shard_map/ppermute | solution.py:669
  74.1 60.1 %collective-permute-start.20 = (bf16[2,384,384]{2,1,0:T(8,128)(2,1)S(1)}, bf16[2,384,384]{2,1,0:T(8,128)(2,1)S(1)}, u32[]{:S(2)}, u32[]{:S(2)}) collective-permute-start(bf16[2,384,384]{2,1,0:T(8,128)(2,1)S(1)} %pad_maximum_fusion.1.refs_8_), channel_id=1, source_target_pairs={{0,4},{1,5},{2,6},{3,7},{4,0},{5,1},{6,2},{7,3},{8,12},{9,13},{10,... | collective-permute-start | bytes 1769480 | tf_op jit(solution)/shard_map/ppermute | solution.py:669
  75.1 59.2 %collective-permute-start.18 = (bf16[2,384,384]{2,1,0:T(8,128)(2,1)S(1)}, bf16[2,384,384]{2,1,0:T(8,128)(2,1)}, u32[]{:S(2)}, u32[]{:S(2)}) collective-permute-start(bf16[2,384,384]{2,1,0:T(8,128)(2,1)S(1)} %pad_maximum_fusion.1.refs_8_), channel_id=1, source_target_pairs={{0,2},{1,3},{2,0},{3,1},{4,6},{5,7},{6,4},{7,5},{8,10},{9,11},{10,... | collective-permute-start | bytes 1769480 | tf_op jit(solution)/shard_map/ppermute | solution.py:669
  81.4 53.4 %collective-permute-start.30 = (bf16[2,96,1536]{2,1,0:T(8,128)(2,1)S(1)}, bf16[2,96,1536]{2,1,0:T(8,128)(2,1)}, u32[]{:S(2)}, u32[]{:S(2)}) collective-permute-start(bf16[2,96,1536]{2,1,0:T(8,128)(2,1)S(1)} %pad_maximum_fusion.2.refs_0_), channel_id=1, source_target_pairs={{0,4},{1,5},{2,6},{3,7},{4,0},{5,1},{6,2},{7,3},{8,12},{9,13},{10,... | collective-permute-start | bytes 1769480 | tf_op jit(solution)/shard_map/ppermute | solution.py:669
  82.9 52.0 %collective-permute-start.11 = (bf16[2,96,1536]{2,1,0:T(8,128)(2,1)S(1)}, bf16[2,96,1536]{2,1,0:T(8,128)(2,1)}, u32[]{:S(2)}, u32[]{:S(2)}) collective-permute-start(bf16[2,96,1536]{2,1,0:T(8,128)(2,1)S(1)} %pad_maximum_fusion.refs_0_), channel_id=1, source_target_pairs={{0,4},{1,5},{2,6},{3,7},{4,0},{5,1},{6,2},{7,3},{8,12},{9,13},{10,... | collective-permute-start | bytes 1769480 | tf_op jit(solution)/shard_map/ppermute | solution.py:669
  94.0 42.4 %collective-permute-start.9 = (bf16[2,96,1536]{2,1,0:T(8,128)(2,1)S(1)}, bf16[2,96,1536]{2,1,0:T(8,128)(2,1)}, u32[]{:S(2)}, u32[]{:S(2)}) collective-permute-start(bf16[2,96,1536]{2,1,0:T(8,128)(2,1)S(1)} %pad_maximum_fusion.refs_0_), channel_id=1, source_target_pairs={{0,2},{1,3},{2,0},{3,1},{4,6},{5,7},{6,4},{7,5},{8,10},{9,11},{10,... | collective-permute-start | bytes 1769480 | tf_op jit(solution)/shard_map/ppermute | solution.py:669
  134.2 37.5 %collective-permute-start.17 = (bf16[2,384,384]{2,1,0:T(8,128)(2,1)S(1)}, bf16[2,384,384]{2,1,0:T(8,128)(2,1)}, u32[]{:S(2)}, u32[]{:S(2)}) collective-permute-start(bf16[2,384,384]{2,1,0:T(8,128)(2,1)S(1)} %pad_maximum_fusion.1.refs_8_), channel_id=1, source_target_pairs={{0,1},{1,0},{2,3},{3,2},{4,5},{5,4},{6,7},{7,6},{8,9},{9,8},{10,11... | collective-permute-start | bytes 1769480 | tf_op jit(solution)/shard_map/ppermute | solution.py:669
  134.3 38.3 %collective-permute-start.27 = (bf16[2,96,1536]{2,1,0:T(8,128)(2,1)S(1)}, bf16[2,96,1536]{2,1,0:T(8,128)(2,1)}, u32[]{:S(2)}, u32[]{:S(2)}) collective-permute-start(bf16[2,96,1536]{2,1,0:T(8,128)(2,1)S(1)} %pad_maximum_fusion.2.refs_0_), channel_id=1, source_target_pairs={{0,1},{1,0},{2,3},{3,2},{4,5},{5,4},{6,7},{7,6},{8,9},{9,8},{10,11... | collective-permute-start | bytes 1769480 | tf_op jit(solution)/shard_map/ppermute | solution.py:669
  134.8 39.0 %collective-permute-start.8 = (bf16[2,96,1536]{2,1,0:T(8,128)(2,1)S(1)}, bf16[2,96,1536]{2,1,0:T(8,128)(2,1)}, u32[]{:S(2)}, u32[]{:S(2)}) collective-permute-start(bf16[2,96,1536]{2,1,0:T(8,128)(2,1)S(1)} %pad_maximum_fusion.refs_0_), channel_id=1, source_target_pairs={{0,1},{1,0},{2,3},{3,2},{4,5},{5,4},{6,7},{7,6},{8,9},{9,8},{10,11... | collective-permute-start | bytes 1769480 | tf_op jit(solution)/shard_map/ppermute | solution.py:669
  134.9 39.7 %collective-permute-start.42 = (bf16[1,384,384]{2,1,0:T(8,128)(2,1)S(1)}, bf16[1,384,384]{2,1,0:T(8,128)(2,1)S(1)}, u32[]{:S(2)}, u32[]{:S(2)}) collective-permute-start(bf16[1,384,384]{2,1,0:T(8,128)(2,1)S(1)} %slice.226), channel_id=1, source_target_pairs={{0,4},{1,5},{2,6},{3,7},{4,0},{5,1},{6,2},{7,3},{8,12},{9,13},{10,... | collective-permute-start | bytes 884744 | tf_op jit(solution)/shard_map/ppermute | solution.py:669
  136.4 38.2 %collective-permute-start.32 = (bf16[1,96,1536]{2,1,0:T(8,128)(2,1)S(1)}, bf16[1,96,1536]{2,1,0:T(8,128)(2,1)S(1)}, u32[]{:S(2)}, u32[]{:S(2)}) collective-permute-start(bf16[1,96,1536]{2,1,0:T(8,128)(2,1)S(1)} %slice.224), channel_id=1, source_target_pairs={{0,4},{1,5},{2,6},{3,7},{4,0},{5,1},{6,2},{7,3},{8,12},{9,13},{10,... | collective-permute-start | bytes 884744 | tf_op jit(solution)/shard_map/ppermute | solution.py:669
  171.7 10.0 %collective-permute-start.43 = (bf16[1,384,384]{2,1,0:T(8,128)(2,1)S(1)}, bf16[1,384,384]{2,1,0:T(8,128)(2,1)S(1)}, u32[]{:S(2)}, u32[]{:S(2)}) collective-permute-start(bf16[1,384,384]{2,1,0:T(8,128)(2,1)S(1)} %slice.227), channel_id=1, source_target_pairs={{0,2},{1,3},{2,0},{3,1},{4,6},{5,7},{6,4},{7,5},{8,10},{9,11},{10,... | collective-permute-start | bytes 884744 | tf_op jit(solution)/shard_map/ppermute | solution.py:669
  172.6 15.4 %collective-permute-start.23 = (bf16[1,384,384]{2,1,0:T(8,128)(2,1)S(1)}, bf16[1,384,384]{2,1,0:T(8,128)(2,1)S(1)}, u32[]{:S(2)}, u32[]{:S(2)}) collective-permute-start(bf16[1,384,384]{2,1,0:T(8,128)(2,1)S(1)} %slice.223), channel_id=1, source_target_pairs={{0,2},{1,3},{2,0},{3,1},{4,6},{5,7},{6,4},{7,5},{8,10},{9,11},{10,... | collective-permute-start | bytes 884744 | tf_op jit(solution)/shard_map/ppermute | solution.py:669
  173.8 20.5 %collective-permute-start.33 = (bf16[1,96,1536]{2,1,0:T(8,128)(2,1)S(1)}, bf16[1,96,1536]{2,1,0:T(8,128)(2,1)S(1)}, u32[]{:S(2)}, u32[]{:S(2)}) collective-permute-start(bf16[1,96,1536]{2,1,0:T(8,128)(2,1)S(1)} %slice.225), channel_id=1, source_target_pairs={{0,2},{1,3},{2,0},{3,1},{4,6},{5,7},{6,4},{7,5},{8,10},{9,11},{10,... | collective-permute-start | bytes 884744 | tf_op jit(solution)/shard_map/ppermute | solution.py:669
  174.6 26.5 %collective-permute-start.41 = (bf16[2,384,384]{2,1,0:T(8,128)(2,1)S(1)}, bf16[2,384,384]{2,1,0:T(8,128)(2,1)S(1)}, u32[]{:S(2)}, u32[]{:S(2)}) collective-permute-start(bf16[2,384,384]{2,1,0:T(8,128)(2,1)S(1)} %copy-done.30), channel_id=1, source_target_pairs={{0,1},{1,0},{2,3},{3,2},{4,5},{5,4},{6,7},{7,6},{8,9},{9,8},{10,11... | collective-permute-start | bytes 1769480 | tf_op jit(solution)/shard_map/ppermute | solution.py:669
  174.6 27.0 %collective-permute-start.39 = (bf16[2,384,384]{2,1,0:T(8,128)(2,1)S(1)}, bf16[2,384,384]{2,1,0:T(8,128)(2,1)S(1)}, u32[]{:S(2)}, u32[]{:S(2)}) collective-permute-start(bf16[2,384,384]{2,1,0:T(8,128)(2,1)S(1)} %copy-done.33), channel_id=1, source_target_pairs={{0,1},{1,0},{2,3},{3,2},{4,5},{5,4},{6,7},{7,6},{8,9},{9,8},{10,11... | collective-permute-start | bytes 1769480 | tf_op jit(solution)/shard_map/ppermute | solution.py:669
  181.6 14.2 %collective-permute-start.22 = (bf16[1,384,384]{2,1,0:T(8,128)(2,1)S(1)}, bf16[1,384,384]{2,1,0:T(8,128)(2,1)S(1)}, u32[]{:S(2)}, u32[]{:S(2)}) collective-permute-start(bf16[1,384,384]{2,1,0:T(8,128)(2,1)S(1)} %slice.222), channel_id=1, source_target_pairs={{0,4},{1,5},{2,6},{3,7},{4,0},{5,1},{6,2},{7,3},{8,12},{9,13},{10,... | collective-permute-start | bytes 884744 | tf_op jit(solution)/shard_map/ppermute | solution.py:669
  188.0 11.5 %collective-permute-start.14 = (bf16[1,96,1536]{2,1,0:T(8,128)(2,1)S(1)}, bf16[1,96,1536]{2,1,0:T(8,128)(2,1)S(1)}, u32[]{:S(2)}, u32[]{:S(2)}) collective-permute-start(bf16[1,96,1536]{2,1,0:T(8,128)(2,1)S(1)} %slice.221), channel_id=1, source_target_pairs={{0,2},{1,3},{2,0},{3,1},{4,6},{5,7},{6,4},{7,5},{8,10},{9,11},{10,... | collective-permute-start | bytes 884744 | tf_op jit(solution)/shard_map/ppermute | solution.py:669
  201.9 60.0 %collective-permute-start.19 = (bf16[2,384,384]{2,1,0:T(8,128)(2,1)}, bf16[2,384,384]{2,1,0:T(8,128)(2,1)S(1)}, u32[]{:S(2)}, u32[]{:S(2)}) collective-permute-start(bf16[2,384,384]{2,1,0:T(8,128)(2,1)} %collective-permute-done.18.refs_10_), channel_id=1, source_target_pairs={{0,1},{1,0},{2,3},{3,2},{4,5},{5,4},{6,7},{7,6},{8,9},{9,8},{10,11... | collective-permute-start | bytes 1769480 | tf_op jit(solution)/shard_map/ppermute | solution.py:669
  202.4 59.6 %collective-permute-start.12 = (bf16[2,96,1536]{2,1,0:T(8,128)(2,1)}, bf16[2,96,1536]{2,1,0:T(8,128)(2,1)S(1)}, u32[]{:S(2)}, u32[]{:S(2)}) collective-permute-start(bf16[2,96,1536]{2,1,0:T(8,128)(2,1)} %collective-permute-done.11.refs_4_), channel_id=1, source_target_pairs={{0,1},{1,0},{2,3},{3,2},{4,5},{5,4},{6,7},{7,6},{8,9},{9,8},{10,11... | collective-permute-start | bytes 1769480 | tf_op jit(solution)/shard_map/ppermute | solution.py:669
  203.1 58.9 %collective-permute-start.10 = (bf16[2,96,1536]{2,1,0:T(8,128)(2,1)}, bf16[2,96,1536]{2,1,0:T(8,128)(2,1)}, u32[]{:S(2)}, u32[]{:S(2)}) collective-permute-start(bf16[2,96,1536]{2,1,0:T(8,128)(2,1)} %collective-permute-done.9.refs_2_), channel_id=1, source_target_pairs={{0,1},{1,0},{2,3},{3,2},{4,5},{5,4},{6,7},{7,6},{8,9},{9,8},{10,11... | collective-permute-start | bytes 1769480 | tf_op jit(solution)/shard_map/ppermute | solution.py:669
  203.9 58.1 %collective-permute-start.24 = (bf16[2,384,384]{2,1,0:T(8,128)(2,1)S(1)}, bf16[2,384,384]{2,1,0:T(8,128)(2,1)S(1)}, u32[]{:S(2)}, u32[]{:S(2)}) collective-permute-start(bf16[2,384,384]{2,1,0:T(8,128)(2,1)S(1)} %constant_dynamic-update-slice_fusion.17.refs_14_), channel_id=1, source_target_pairs={{0,1},{1,0},{2,3},{3,2},{4,5},{5,4},{6,7},{7,6},{8,9},{9,8},{10,11... | collective-permute-start | bytes 1769480 | tf_op jit(solution)/shard_map/ppermute | solution.py:669
  205.6 56.4 %collective-permute-start.15 = (bf16[2,96,1536]{2,1,0:T(8,128)(2,1)S(1)}, bf16[2,96,1536]{2,1,0:T(8,128)(2,1)}, u32[]{:S(2)}, u32[]{:S(2)}) collective-permute-start(bf16[2,96,1536]{2,1,0:T(8,128)(2,1)S(1)} %constant_dynamic-update-slice_fusion.15.refs_6_), channel_id=1, source_target_pairs={{0,1},{1,0},{2,3},{3,2},{4,5},{5,4},{6,7},{7,6},{8,9},{9,8},{10,11... | collective-permute-start | bytes 1769480 | tf_op jit(solution)/shard_map/ppermute | solution.py:669
  412.5 12.0 %collective-permute-start.62 = (bf16[2,96,1536]{2,1,0:T(8,128)(2,1)}, bf16[2,96,1536]{2,1,0:T(8,128)(2,1)S(1)}, u32[]{:S(2)}, u32[]{:S(2)}) collective-permute-start(bf16[2,96,1536]{2,1,0:T(8,128)(2,1)} %get-tuple-element.90), channel_id=1, source_target_pairs={{0,1},{1,0},{2,3},{3,2},{4,5},{5,4},{6,7},{7,6},{8,9},{9,8},{10,11... | collective-permute-start | bytes 1769480 | tf_op jit(solution)/shard_map/ppermute | solution.py:669
  421.6 56.3 %collective-permute-start.61 = (bf16[2,96,1536]{2,1,0:T(8,128)(2,1)}, bf16[2,96,1536]{2,1,0:T(8,128)(2,1)}, u32[]{:S(2)}, u32[]{:S(2)}) collective-permute-start(bf16[2,96,1536]{2,1,0:T(8,128)(2,1)} %get-tuple-element.88), channel_id=1, source_target_pairs={{0,1},{1,0},{2,3},{3,2},{4,5},{5,4},{6,7},{7,6},{8,9},{9,8},{10,11... | collective-permute-start | bytes 1769480 | tf_op jit(solution)/shard_map/ppermute | solution.py:669
  424.5 69.6 %collective-permute-start.80 = (bf16[2,384,384]{2,1,0:T(8,128)(2,1)}, bf16[2,384,384]{2,1,0:T(8,128)(2,1)S(1)}, u32[]{:S(2)}, u32[]{:S(2)}) collective-permute-start(bf16[2,384,384]{2,1,0:T(8,128)(2,1)} %get-tuple-element.104), channel_id=1, source_target_pairs={{0,1},{1,0},{2,3},{3,2},{4,5},{5,4},{6,7},{7,6},{8,9},{9,8},{10,11... | collective-permute-start | bytes 1769480 | tf_op jit(solution)/shard_map/ppermute | solution.py:669
  441.6 13.1 %collective-permute-start.64 = (bf16[1,96,1536]{2,1,0:T(8,128)(2,1)S(1)}, bf16[1,96,1536]{2,1,0:T(8,128)(2,1)S(1)}, u32[]{:S(2)}, u32[]{:S(2)}) collective-permute-start(bf16[1,96,1536]{2,1,0:T(8,128)(2,1)S(1)} %get-tuple-element.142), channel_id=1, source_target_pairs={{0,4},{1,5},{2,6},{3,7},{4,0},{5,1},{6,2},{7,3},{8,12},{9,13},{10,... | collective-permute-start | bytes 884744 | tf_op jit(solution)/shard_map/ppermute | solution.py:669
  445.2 10.6 %collective-permute-start.67 = (bf16[1,96,1536]{2,1,0:T(8,128)(2,1)S(1)}, bf16[1,96,1536]{2,1,0:T(8,128)(2,1)S(1)}, u32[]{:S(2)}, u32[]{:S(2)}) collective-permute-start(bf16[1,96,1536]{2,1,0:T(8,128)(2,1)S(1)} %get-tuple-element.143), channel_id=1, source_target_pairs={{0,2},{1,3},{2,0},{3,1},{4,6},{5,7},{6,4},{7,5},{8,10},{9,11},{10,... | collective-permute-start | bytes 884744 | tf_op jit(solution)/shard_map/ppermute | solution.py:669
  448.4 12.6 %collective-permute-start.83 = (bf16[1,384,384]{2,1,0:T(8,128)(2,1)S(1)}, bf16[1,384,384]{2,1,0:T(8,128)(2,1)S(1)}, u32[]{:S(2)}, u32[]{:S(2)}) collective-permute-start(bf16[1,384,384]{2,1,0:T(8,128)(2,1)S(1)} %get-tuple-element.136), channel_id=1, source_target_pairs={{0,4},{1,5},{2,6},{3,7},{4,0},{5,1},{6,2},{7,3},{8,12},{9,13},{10,... | collective-permute-start | bytes 884744 | tf_op jit(solution)/shard_map/ppermute | solution.py:669
  454.7 12.9 %collective-permute-start.86 = (bf16[1,384,384]{2,1,0:T(8,128)(2,1)S(1)}, bf16[1,384,384]{2,1,0:T(8,128)(2,1)S(1)}, u32[]{:S(2)}, u32[]{:S(2)}) collective-permute-start(bf16[1,384,384]{2,1,0:T(8,128)(2,1)S(1)} %get-tuple-element.137), channel_id=1, source_target_pairs={{0,2},{1,3},{2,0},{3,1},{4,6},{5,7},{6,4},{7,5},{8,10},{9,11},{10,... | collective-permute-start | bytes 884744 | tf_op jit(solution)/shard_map/ppermute | solution.py:669
  455.8 11.0 %collective-permute-start.55 = (bf16[1,96,1536]{2,1,0:T(8,128)(2,1)S(1)}, bf16[1,96,1536]{2,1,0:T(8,128)(2,1)S(1)}, u32[]{:S(2)}, u32[]{:S(2)}) collective-permute-start(bf16[1,96,1536]{2,1,0:T(8,128)(2,1)S(1)} %get-tuple-element.138), channel_id=1, source_target_pairs={{0,4},{1,5},{2,6},{3,7},{4,0},{5,1},{6,2},{7,3},{8,12},{9,13},{10,... | collective-permute-start | bytes 884744 | tf_op jit(solution)/shard_map/ppermute | solution.py:669
  467.7 10.0 %collective-permute-start.77 = (bf16[1,384,384]{2,1,0:T(8,128)(2,1)S(1)}, bf16[1,384,384]{2,1,0:T(8,128)(2,1)S(1)}, u32[]{:S(2)}, u32[]{:S(2)}) collective-permute-start(bf16[1,384,384]{2,1,0:T(8,128)(2,1)S(1)} %get-tuple-element.133), channel_id=1, source_target_pairs={{0,2},{1,3},{2,0},{3,1},{4,6},{5,7},{6,4},{7,5},{8,10},{9,11},{10,... | collective-permute-start | bytes 884744 | tf_op jit(solution)/shard_map/ppermute | solution.py:669
  468.9 21.4 %collective-permute-start.65 = (bf16[2,96,1536]{2,1,0:T(8,128)(2,1)S(1)}, bf16[2,96,1536]{2,1,0:T(8,128)(2,1)S(1)}, u32[]{:S(2)}, u32[]{:S(2)}) collective-permute-start(bf16[2,96,1536]{2,1,0:T(8,128)(2,1)S(1)} %pad_maximum_fusion.6), channel_id=1, source_target_pairs={{0,2},{1,3},{2,0},{3,1},{4,6},{5,7},{6,4},{7,5},{8,10},{9,11},{10,... | collective-permute-start | bytes 1769480 | tf_op jit(solution)/shard_map/ppermute | solution.py:669
  475.2 16.5 %collective-permute-start.68 = (bf16[2,96,1536]{2,1,0:T(8,128)(2,1)S(1)}, bf16[2,96,1536]{2,1,0:T(8,128)(2,1)S(1)}, u32[]{:S(2)}, u32[]{:S(2)}) collective-permute-start(bf16[2,96,1536]{2,1,0:T(8,128)(2,1)S(1)} %pad_maximum_fusion.7), channel_id=1, source_target_pairs={{0,4},{1,5},{2,6},{3,7},{4,0},{5,1},{6,2},{7,3},{8,12},{9,13},{10,... | collective-permute-start | bytes 1769480 | tf_op jit(solution)/shard_map/ppermute | solution.py:669
  477.7 30.2 %collective-permute-start.52 = (bf16[2,96,1536]{2,1,0:T(8,128)(2,1)S(1)}, bf16[2,96,1536]{2,1,0:T(8,128)(2,1)S(1)}, u32[]{:S(2)}, u32[]{:S(2)}) collective-permute-start(bf16[2,96,1536]{2,1,0:T(8,128)(2,1)S(1)} %copy-done.43), channel_id=1, source_target_pairs={{0,1},{1,0},{2,3},{3,2},{4,5},{5,4},{6,7},{7,6},{8,9},{9,8},{10,11... | collective-permute-start | bytes 1769480 | tf_op jit(solution)/shard_map/ppermute | solution.py:669
  477.8 25.1 %collective-permute-start.84 = (bf16[2,384,384]{2,1,0:T(8,128)(2,1)S(1)}, bf16[2,384,384]{2,1,0:T(8,128)(2,1)S(1)}, u32[]{:S(2)}, u32[]{:S(2)}) collective-permute-start(bf16[2,384,384]{2,1,0:T(8,128)(2,1)S(1)} %pad_maximum_fusion.10), channel_id=1, source_target_pairs={{0,2},{1,3},{2,0},{3,1},{4,6},{5,7},{6,4},{7,5},{8,10},{9,11},{10,... | collective-permute-start | bytes 1769480 | tf_op jit(solution)/shard_map/ppermute | solution.py:669
  490.3 16.3 %collective-permute-start.87 = (bf16[2,384,384]{2,1,0:T(8,128)(2,1)S(1)}, bf16[2,384,384]{2,1,0:T(8,128)(2,1)S(1)}, u32[]{:S(2)}, u32[]{:S(2)}) collective-permute-start(bf16[2,384,384]{2,1,0:T(8,128)(2,1)S(1)} %pad_maximum_fusion.11), channel_id=1, source_target_pairs={{0,4},{1,5},{2,6},{3,7},{4,0},{5,1},{6,2},{7,3},{8,12},{9,13},{10,... | collective-permute-start | bytes 1769480 | tf_op jit(solution)/shard_map/ppermute | solution.py:669
  491.7 23.9 %collective-permute-start.56 = (bf16[2,96,1536]{2,1,0:T(8,128)(2,1)S(1)}, bf16[2,96,1536]{2,1,0:T(8,128)(2,1)S(1)}, u32[]{:S(2)}, u32[]{:S(2)}) collective-permute-start(bf16[2,96,1536]{2,1,0:T(8,128)(2,1)S(1)} %pad_maximum_fusion.4), channel_id=1, source_target_pairs={{0,2},{1,3},{2,0},{3,1},{4,6},{5,7},{6,4},{7,5},{8,10},{9,11},{10,... | collective-permute-start | bytes 1769480 | tf_op jit(solution)/shard_map/ppermute | solution.py:669
  494.1 25.1 %collective-permute-start.59 = (bf16[2,96,1536]{2,1,0:T(8,128)(2,1)S(1)}, bf16[2,96,1536]{2,1,0:T(8,128)(2,1)S(1)}, u32[]{:S(2)}, u32[]{:S(2)}) collective-permute-start(bf16[2,96,1536]{2,1,0:T(8,128)(2,1)S(1)} %pad_maximum_fusion.5), channel_id=1, source_target_pairs={{0,4},{1,5},{2,6},{3,7},{4,0},{5,1},{6,2},{7,3},{8,12},{9,13},{10,... | collective-permute-start | bytes 1769480 | tf_op jit(solution)/shard_map/ppermute | solution.py:669
  503.0 19.9 %collective-permute-start.71 = (bf16[2,384,384]{2,1,0:T(8,128)(2,1)S(1)}, bf16[2,384,384]{2,1,0:T(8,128)(2,1)S(1)}, u32[]{:S(2)}, u32[]{:S(2)}) collective-permute-start(bf16[2,384,384]{2,1,0:T(8,128)(2,1)S(1)} %copy-done.42), channel_id=1, source_target_pairs={{0,1},{1,0},{2,3},{3,2},{4,5},{5,4},{6,7},{7,6},{8,9},{9,8},{10,11... | collective-permute-start | bytes 1769480 | tf_op jit(solution)/shard_map/ppermute | solution.py:669
  506.6 20.0 %collective-permute-start.75 = (bf16[2,384,384]{2,1,0:T(8,128)(2,1)S(1)}, bf16[2,384,384]{2,1,0:T(8,128)(2,1)S(1)}, u32[]{:S(2)}, u32[]{:S(2)}) collective-permute-start(bf16[2,384,384]{2,1,0:T(8,128)(2,1)S(1)} %pad_maximum_fusion.8), channel_id=1, source_target_pairs={{0,2},{1,3},{2,0},{3,1},{4,6},{5,7},{6,4},{7,5},{8,10},{9,11},{10,... | collective-permute-start | bytes 1769480 | tf_op jit(solution)/shard_map/ppermute | solution.py:669
  507.9 19.6 %collective-permute-start.78 = (bf16[2,384,384]{2,1,0:T(8,128)(2,1)S(1)}, bf16[2,384,384]{2,1,0:T(8,128)(2,1)S(1)}, u32[]{:S(2)}, u32[]{:S(2)}) collective-permute-start(bf16[2,384,384]{2,1,0:T(8,128)(2,1)S(1)} %pad_maximum_fusion.9), channel_id=1, source_target_pairs={{0,4},{1,5},{2,6},{3,7},{4,0},{5,1},{6,2},{7,3},{8,12},{9,13},{10,... | collective-permute-start | bytes 1769480 | tf_op jit(solution)/shard_map/ppermute | solution.py:669
  515.6 15.8 %collective-permute-start.49 = (bf16[48,384]{1,0:T(8,128)(2,1)S(1)}, bf16[48,384]{1,0:T(8,128)(2,1)S(1)}, u32[]{:S(2)}, u32[]{:S(2)}) collective-permute-start(bf16[48,384]{1,0:T(8,128)(2,1)S(1)} %get-tuple-element.147), channel_id=1, source_target_pairs={{0,8},{1,9},{2,10},{3,11},{4,12},{5,13},{6,14},{7,15},{8,0},{9,1},... | collective-permute-start | bytes 110600 | tf_op jit(solution)/shard_map/ppermute | solution.py:669
  519.2 12.3 %collective-permute-start.51 = (bf16[48,384]{1,0:T(8,128)(2,1)S(1)}, bf16[48,384]{1,0:T(8,128)(2,1)S(1)}, u32[]{:S(2)}, u32[]{:S(2)}) collective-permute-start(bf16[48,384]{1,0:T(8,128)(2,1)S(1)} %get-tuple-element.148), channel_id=1, source_target_pairs={{0,24},{1,25},{2,26},{3,27},{4,28},{5,29},{6,30},{7,31},{8,16},{9,... | collective-permute-start | bytes 110600 | tf_op jit(solution)/shard_map/ppermute | solution.py:669
  522.9 9.6 %collective-permute-start.50 = (bf16[48,384]{1,0:T(8,128)(2,1)S(1)}, bf16[48,384]{1,0:T(8,128)(2,1)S(1)}, u32[]{:S(2)}, u32[]{:S(2)}) collective-permute-start(bf16[48,384]{1,0:T(8,128)(2,1)S(1)} %get-tuple-element.149), channel_id=1, source_target_pairs={{0,16},{1,17},{2,18},{3,19},{4,20},{5,21},{6,22},{7,23},{8,24},{9,... | collective-permute-start | bytes 110600 | tf_op jit(solution)/shard_map/ppermute | solution.py:669
  526.5 32.4 %collective-permute-start.88 = (bf16[384,384]{1,0:T(8,128)(2,1)S(1)}, bf16[384,384]{1,0:T(8,128)(2,1)S(1)}, u32[]{:S(2)}, u32[]{:S(2)}) collective-permute-start(bf16[384,384]{1,0:T(8,128)(2,1)S(1)} %get-tuple-element.134), channel_id=1, source_target_pairs={{0,16},{1,17},{2,18},{3,19},{4,20},{5,21},{6,22},{7,23},{8,24},{9,... | collective-permute-start | bytes 884744 | tf_op jit(solution)/shard_map/ppermute | solution.py:669
  527.6 32.1 %collective-permute-start.89 = (bf16[384,384]{1,0:T(8,128)(2,1)S(1)}, bf16[384,384]{1,0:T(8,128)(2,1)S(1)}, u32[]{:S(2)}, u32[]{:S(2)}) collective-permute-start(bf16[384,384]{1,0:T(8,128)(2,1)S(1)} %get-tuple-element.135), channel_id=1, source_target_pairs={{0,24},{1,25},{2,26},{3,27},{4,28},{5,29},{6,30},{7,31},{8,16},{9,... | collective-permute-start | bytes 884744 | tf_op jit(solution)/shard_map/ppermute | solution.py:669
  531.4 28.2 %collective-permute-start.79 = (bf16[384,384]{1,0:T(8,128)(2,1)S(1)}, bf16[384,384]{1,0:T(8,128)(2,1)S(1)}, u32[]{:S(2)}, u32[]{:S(2)}) collective-permute-start(bf16[384,384]{1,0:T(8,128)(2,1)S(1)} %slice_bitcast_fusion.2), channel_id=1, source_target_pairs={{0,8},{1,9},{2,10},{3,11},{4,12},{5,13},{6,14},{7,15},{8,0},{9,1},... | collective-permute-start | bytes 884744 | tf_op jit(solution)/shard_map/ppermute | solution.py:669
  531.5 42.2 %collective-permute-start.69 = (bf16[96,1536]{1,0:T(8,128)(2,1)S(1)}, bf16[96,1536]{1,0:T(8,128)(2,1)S(1)}, u32[]{:S(2)}, u32[]{:S(2)}) collective-permute-start(bf16[96,1536]{1,0:T(8,128)(2,1)S(1)} %get-tuple-element.140), channel_id=1, source_target_pairs={{0,16},{1,17},{2,18},{3,19},{4,20},{5,21},{6,22},{7,23},{8,24},{9,... | collective-permute-start | bytes 884744 | tf_op jit(solution)/shard_map/ppermute | solution.py:669
  532.5 41.2 %collective-permute-start.70 = (bf16[96,1536]{1,0:T(8,128)(2,1)S(1)}, bf16[96,1536]{1,0:T(8,128)(2,1)S(1)}, u32[]{:S(2)}, u32[]{:S(2)}) collective-permute-start(bf16[96,1536]{1,0:T(8,128)(2,1)S(1)} %get-tuple-element.141), channel_id=1, source_target_pairs={{0,24},{1,25},{2,26},{3,27},{4,28},{5,29},{6,30},{7,31},{8,16},{9,... | collective-permute-start | bytes 884744 | tf_op jit(solution)/shard_map/ppermute | solution.py:669
  559.0 14.8 %collective-permute-start.60 = (bf16[96,1536]{1,0:T(8,128)(2,1)S(1)}, bf16[96,1536]{1,0:T(8,128)(2,1)S(1)}, u32[]{:S(2)}, u32[]{:S(2)}) collective-permute-start(bf16[96,1536]{1,0:T(8,128)(2,1)S(1)} %slice_bitcast_fusion.6), channel_id=1, source_target_pairs={{0,8},{1,9},{2,10},{3,11},{4,12},{5,13},{6,14},{7,15},{8,0},{9,1},... | collective-permute-start | bytes 884744 | tf_op jit(solution)/shard_map/ppermute | solution.py:669
  (101 other events, 1209.9 us)
